TPU v7x, 32 devices: a whole 2x2x4 slice. The times are simulated.
32 devices in a mesh: groups: 1, pair: 32 (over z, y, x, core), coef: 1.
Axes of the slice: x: 2, y: 2, z: 4, core: 2. Of those that a mesh axis runs over, the one named last changes fastest.
Arguments:
- tiles: bfloat16 [256, 64, 64, 64], P(('pair', 'coef')), may hold values from -6 to 6
- occ_coef: bfloat16 [3968, 32], P('coef', 'groups'), may hold values from -0.75 to 0.75
- vir_coef: bfloat16 [3968, 3072], P('pair', 'coef'), may hold values from -0.09375 to 0.09375
- shell_pairs: int32 [2, 256], replicated, may hold values from 0 to 61
- live_flags: int32 [256], replicated, may hold values from 0 to 1, as said below
Outputs:
- mo_ints: bfloat16 [64, 32, 3072], P('pair', 'groups', 'coef')
Inputs may be any that keep to these rules, and one draw needn't show every extreme that they name: `live_flags`: among the 8 slots of one device (aligned blocks of 8 entries) at least one and at most 4 flags are 1; some device has exactly 4.
All inputs are finite; a program needn't handle non-finite values.
Results may differ from a plain program's by a relative error of at most 0.0049.
Values may be sent and summed in bfloat16 or wider, within the bound.
No kernel may reach another device: no remote copies, remote signals or barrier semaphores. Data moves between devices by JAX's collectives and lax.ppermute only.
A program may use at most 128 MiB of HBM per device.

v0:
```python
import jax
import jax.numpy as jnp
from jax import lax
from jax.sharding import PartitionSpec as P


def on_device(tiles, occ_coef, vir_coef, shell_pairs, live_flags):
    slot_count, shell_size, unused_dim, ket_cols = tiles.shape
    pair_count = lax.axis_size("pair")
    coef_count = lax.axis_size("coef")
    core_index = lax.axis_index("coef")
    device_index = lax.axis_index(("pair", "coef"))
    occ_full = lax.all_gather(occ_coef, "coef", axis=0, tiled=True)
    basis_count, occ_count = occ_full.shape
    shell_count = basis_count // shell_size
    ket_owned = ket_cols // pair_count
    occ_shells = occ_full.reshape(shell_count, shell_size, occ_count)
    block_table = shell_pairs.reshape(2, pair_count * coef_count, slot_count)
    flag_table = live_flags.reshape(pair_count * coef_count, slot_count)
    own_mu = lax.dynamic_index_in_dim(block_table[0], device_index, 0, keepdims=False)
    own_flag = lax.dynamic_index_in_dim(flag_table, device_index, 0, keepdims=False)
    peer_nu = lax.dynamic_index_in_dim(
        block_table[1].reshape(pair_count, coef_count, slot_count), core_index, 1, keepdims=False
    )
    panels = jnp.take(occ_shells, own_mu, axis=0)
    result = jnp.einsum("bmi,bmnk->bkin", panels, tiles, preferred_element_type=jnp.float32)
    result = result * own_flag.astype(jnp.float32)[:, None, None, None]
    quarter = result.reshape(tiles.shape[0], ket_cols, occ_count * shell_size)
    received = lax.all_to_all(quarter, "pair", split_axis=1, concat_axis=0, tiled=True)
    recv_shells = peer_nu.reshape(-1)
    selector = (jnp.arange(shell_count, dtype=jnp.int32)[:, None] == recv_shells[None, :]).astype(
        jnp.float32
    )
    received = received.reshape(-1, ket_owned, occ_count, shell_size)
    partial_sum = jnp.einsum("gb,bkis->kigs", selector, received, precision=lax.Precision.HIGHEST)
    half_sum = lax.psum(partial_sum, "coef")
    half_ints = half_sum.reshape(ket_owned * occ_count, basis_count).astype(jnp.bfloat16)
    result = jnp.dot(
        half_ints,
        lax.all_gather(vir_coef, "pair", axis=0, tiled=True),
        preferred_element_type=jnp.float32,
    )
    return result.reshape(ket_owned, occ_count, vir_coef.shape[1]).astype(jnp.bfloat16)


def solution(mesh):
    in_specs = (
        P(("pair", "coef"), None, None, None),
        P("coef", "groups"),
        P("pair", "coef"),
        P(),
        P(),
    )
    out_specs = P("pair", "groups", "coef")
    return jax.shard_map(
        on_device, mesh=mesh, in_specs=in_specs, out_specs=out_specs, check_vma=False
    )
```

profile of v0, /device:TPU:0, one launch (start us, length us, event | category | flops | bytes accessed | tf_op | source)
XLA Modules:
  0.0 299.3 jit_solution(566117336468952789)
XLA Ops:
  6.5 0.0 all-gather.3.cloned.1.call-start
  6.5 0.7 all-gather.3.cloned.1.call-update
  7.3 0.8 fusion.21
  8.0 0.1 squeeze.12
  8.1 0.8 reshape.66
  8.9 1.5 reshape.65
  10.3 0.3 copy.14
  10.7 0.6 gather_fusion
  11.3 12.7 %multiply_bitcast_fusion = f32[8,64,32,64]{1,2,3,0:T(8,128)} fusion(f32[8]{0:T(128)S(1)} %convert_bitcast_fusion, bf16[8,64,64,64]{3,2,1,0:T(8,128)(2,1)} %param.5, bf16[8,64,32]{1,2,0:T(8,128)(2,1)S(1)} %gather_fusion, pred[8]{0:T(512)(128)(4,1)S(1)} %compare_and_fusion), kind=kOutput, calls=%fused_computation.5 | convolution fusion | flops 135282688 | bytes 8421416 | tf_op jit(solution)/shard_map/bmi,bmnk->bkin/dot_general | solution.py:26
  24.1 10.3 %copy.23 = f32[8,64,32,64]{3,2,0,1:T(8,128)} copy(f32[8,64,32,64]{1,2,3,0:T(8,128)} %multiply_bitcast_fusion) | data formatting | bytes 8388608 | tf_op jit(solution)/shard_map/reshape | solution.py:28
  34.3 7.8 %reshape.82 = f32[8,64,2048]{2,0,1:T(8,128)} reshape(f32[8,64,32,64]{3,2,0,1:T(8,128)} %copy.23) | data formatting | bytes 8388608 | tf_op jit(solution)/shard_map/reshape | solution.py:28
  42.2 190.9 %all_to_all.15 = f32[8,64,2048]{2,0,1:T(8,128)S(1)} all-to-all(f32[8,64,2048]{2,0,1:T(8,128)} %reshape.82), channel_id=1, replica_groups=mesh['groups'=1,'pair'=32,'coef'=1] {'pair'}, dimensions={1} | all-to-all | bytes 8388608 | tf_op jit(solution)/shard_map/all_to_all | solution.py:29
  233.1 2.3 copy.18
  235.4 7.9 %reshape.68 = f32[256,2,32,64]{3,2,0,1:T(8,128)} reshape(f32[32,8,2,2048]{3,1,0,2:T(8,128)} %copy.18) | data formatting | bytes 8388608 | tf_op jit(solution)/shard_map/reshape | solution.py:34
  243.3 13.2 %fusion.9 = bf16[2,32,62,64]{2,3,1,0:T(8,128)(2,1)S(1)} fusion(f32[256,2,32,64]{3,2,0,1:T(8,128)} %reshape.68, s32[256]{0:T(256)S(1)} %bitcast.41), kind=kOutput, calls=%fused_computation.8 | convolution fusion | flops 780410368 | bytes 4703232 | tf_op jit(solution)/shard_map/gb,bkis->kigs/dot_general | solution.py:35
  256.5 0.8 copy.20
  257.3 0.8 convert_element_type.28
  258.1 0.0 all-gather.3.cloned.1.call-done
  258.1 23.3 %reshape.81 = bf16[3968,3072,1]{1,0,2:T(8,128)(2,1)} reshape(bf16[32,124,3072]{2,1,0:T(8,128)(2,1)} %all-gather.3.cloned.1.call-done) | data formatting | bytes 48758784
  281.4 11.0 %convolution_convert_fusion = bf16[2,32,3072]{2,1,0:T(8,128)(2,1)} fusion(bf16[2,32,3968]{2,1,0:T(8,128)(2,1)S(1)} %convert_element_type.28, bf16[3968,3072,1]{1,0,2:T(8,128)(2,1)} %reshape.81), kind=kOutput, calls=%fused_computation.6 | convolution fusion | flops 1560477696 | bytes 25280512 | tf_op jit(solution)/shard_map/dot_general | solution.py:38
  (4 shorter events, 0.0 us)
Async XLA Ops:
  6.5 251.6 %all-gather.3.cloned.1.call-start = ((), (), s32[]{:S(2)}) async-start(), calls=%async_computation.1 | async-start | bytes 25952256 | tf_op jit(solution)/shard_map/all_gather | solution.py:40
Sparse Core Ops, SparseCore 0:
  10.2 234.6 all-gather.2
where the time goes:
time: 300 us; the launch traced here: 299 us
  blocking collectives  191 us (64%)
  local copies, waits for them, and re-layouts  57.1 us (19%)
  matrix products  36.9 us (12%)
  between operations  13.5 us (4%)
    all_to_all x1, blocking collectives, on_device(): lax.all_to_all(quarter, 'pair', split_axis=1, concat_axis=0, tiled=True)  191 us
    unnamed x1, local copies, waits for them, and re-layouts  23.3 us
    reshape x2, local copies, waits for them, and re-layouts, on_device(): quarter = result.reshape(tiles.shape[0], ket_cols, occ_count * shell_size)  18.1 us
    dot_general x1, matrix products, on_device(): jnp.einsum('gb,bkis->kigs', selector, received, precision=lax.Precision.H...  13.2 us
    dot_general x1, matrix products, on_device(): jnp.einsum('bmi,bmnk->bkin', panels, tiles, preferred_element_type=jnp.fl...  12.7 us
    dot_general x1, matrix products, on_device(): jnp.dot(half_ints, lax.all_gather(vir_coef, 'pair', axis=0, tiled=True),...  11 us
    reshape x1, local copies, waits for them, and re-layouts, on_device(): received = received.reshape(-1, ket_owned, occ_count, shell_size)  7.88 us
  transfers between devices with their start and end apart: 1, of which 0 were waited for; matrix products, arithmetic and copies ran while one was open for 20% of the time, Pallas kernels for 0%

commit v1 on v0

--- a/solution.py
+++ b/solution.py
@@ -1,10 +1,16 @@
 import jax
 import jax.numpy as jnp
 from jax import lax
-from jax.sharding import PartitionSpec as P
-
-
-def on_device(tiles, occ_coef, vir_coef, shell_pairs, live_flags):
+from jax.experimental import pallas as pl
+from jax.experimental.pallas import tpu as pltpu
+from jax.sharding import Mesh, PartitionSpec as P
+
+LIVE = 4
+FAR, NEAR, ROW, COL, CORE = "far", "near", "row", "col", "core"
+AXES = (FAR, NEAR, ROW, COL, CORE)
+
+
+def plain(tiles, occ_coef, vir_coef, shell_pairs, live_flags):
     slot_count, shell_size, unused_dim, ket_cols = tiles.shape
     pair_count = lax.axis_size("pair")
     coef_count = lax.axis_size("coef")
@@ -43,7 +49,216 @@
     return result.reshape(ket_owned, occ_count, vir_coef.shape[1]).astype(jnp.bfloat16)
 
 
+def first_quarter_body(me_ref, flag_ref, pair_ref, occ_ref, tiles_ref, out_ref, held, turned, wide, sem, *, slots):
+    live, shell_size, unused_dim, ket_cols = held.shape
+    occ_count = occ_ref.shape[0]
+    owners, groups, rows, lanes = out_ref.shape
+    step = 16
+    first = me_ref[0] * slots
+    seen = jnp.int32(0)
+    picks = [jnp.int32(0)] * live
+    for slot in range(slots):
+        flag = flag_ref[first + slot]
+        picks = [jnp.where((flag == 1) & (seen == j), slot, pick) for j, pick in enumerate(picks)]
+        seen = seen + flag
+    copies = [
+        pltpu.make_async_copy(tiles_ref.at[pick], held.at[j], sem.at[j]) for j, pick in enumerate(picks)
+    ]
+    for copy in copies:
+        copy.start()
+    inner = shell_size * step
+    spread = (
+        lax.broadcasted_iota(jnp.int32, (shell_size, inner), 1) // step
+        == lax.broadcasted_iota(jnp.int32, (shell_size, inner), 0)
+    ).astype(jnp.bfloat16)
+    diagonal = lax.broadcasted_iota(jnp.int32, (step, inner), 1) % step == lax.broadcasted_iota(
+        jnp.int32, (step, inner), 0
+    )
+    for j in range(live):
+        mu = pair_ref[0, first + picks[j]]
+        both = occ_ref[:, pl.ds(pl.multiple_of(lax.div(mu, 2) * 128, 128), 128)].astype(jnp.float32)
+        both = jnp.where(lax.rem(mu, 2) == 1, pltpu.roll(both, shell_size, 1), both)
+        panel = both[:, :shell_size].astype(jnp.bfloat16)
+        panel = jnp.dot(panel, spread, preferred_element_type=jnp.float32)
+        weight = jnp.where(diagonal[None], panel[:, None, :], 0.0).astype(jnp.bfloat16)
+        weight = weight.reshape(occ_count * step, inner)
+        copies[j].wait()
+        for part in range(shell_size // step):
+            block = held[j, :, part * step : (part + 1) * step, :].reshape(inner, ket_cols)
+            result = jnp.dot(weight, block, preferred_element_type=jnp.float32)
+            turned[j % 2, :, part * step : (part + 1) * step, :] = result.reshape(occ_count, step, ket_cols)
+        if j % 2 == 1:
+            for i in range(occ_count):
+                value = turned[:, i].reshape(2 * shell_size, ket_cols)
+                wide[pl.ds(i, ket_cols, stride=occ_count), :] = value.T
+            out_ref[:, j // 2] = wide[...].astype(jnp.bfloat16).reshape(owners, rows, lanes)
+
+
+def first_quarter(me, flags, pairs, occ, tiles, owners):
+    slots, shell_size, unused_dim, ket_cols = tiles.shape
+    occ_count = occ.shape[0]
+    rows = ket_cols // owners * occ_count
+    shape = (owners, LIVE // 2, rows, 2 * shell_size)
+
+    def body(*refs):
+        first_quarter_body(*refs, slots=slots)
+
+    return pl.pallas_call(
+        body,
+        out_shape=jax.ShapeDtypeStruct(shape, jnp.bfloat16),
+        in_specs=[pl.BlockSpec(memory_space=pltpu.SMEM)] * 3
+        + [pl.BlockSpec(memory_space=pltpu.VMEM), pl.BlockSpec(memory_space=pl.ANY)],
+        out_specs=pl.BlockSpec(memory_space=pltpu.VMEM),
+        scratch_shapes=[
+            pltpu.VMEM((LIVE, shell_size, shell_size, ket_cols), jnp.bfloat16),
+            pltpu.VMEM((2, occ_count, shell_size, ket_cols), jnp.float32),
+            pltpu.VMEM((ket_cols * occ_count, 2 * shell_size), jnp.float32),
+            pltpu.SemaphoreType.DMA((LIVE,)),
+        ],
+        compiler_params=pltpu.CompilerParams(vmem_limit_bytes=32 * 1024 * 1024),
+        cost_estimate=pl.CostEstimate(flops=10**9, bytes_accessed=6 * 10**6, transcendentals=0),
+        name="first_quarter",
+    )(me, flags, pairs, occ, tiles)
+
+
+def sum_shells_body(nu_ref, at_ref, got_ref, out_ref, acc_ref, *, shell_size, depth, blocks):
+    tile_count, rows, lanes = acc_ref.shape
+    per = lanes // shell_size
+    sources, groups = got_ref.shape[0], got_ref.shape[1]
+    acc_ref[...] = jnp.zeros_like(acc_ref)
+    lane = lax.broadcasted_iota(jnp.int32, (rows, lanes), 1)
+
+    def add(source, carry):
+        for group in range(groups):
+            both = got_ref[source, group].astype(jnp.float32)
+            turned = pltpu.roll(both, shell_size, 1)
+            for part in range(per):
+                shell = nu_ref[source * groups * per + group * per + part]
+                place = lax.rem(shell, per)
+                value = jnp.where(place == part, both, turned)
+                value = jnp.where(lane // shell_size == place, value, 0.0)
+                at = lax.div(shell, per)
+                acc_ref[at] = acc_ref[at] + value
+        return carry
+
+    lax.fori_loop(0, sources, add, 0)
+    far, col = at_ref[0], at_ref[1]
+    for block in range(blocks):
+        first = block * depth
+        tile, shift = first // lanes, first % lanes
+        turn = (lanes - shift) % lanes
+        value = acc_ref[tile]
+        if turn:
+            value = pltpu.roll(value, turn, 1)
+            if shift + depth > lanes:
+                value = jnp.where(lane < turn, value, pltpu.roll(acc_ref[tile + 1], turn, 1))
+        value = jnp.where(lane < depth, value, 0.0).astype(out_ref.dtype)
+        bits = [(block >> b) & 1 for b in (4, 3, 2, 1, 0)]
+        spot = 4 * jnp.bitwise_xor(far, bits[0]) + 2 * jnp.bitwise_xor(col, bits[3])
+        for core in range(2):
+            out_ref[4 * bits[1] + 2 * bits[2] + core, spot + (bits[4] ^ core)] = value
+
+
+def sum_shells(nu, at, got, shell_size, shell_count, depth):
+    sources, groups, rows, lanes = got.shape
+    per = lanes // shell_size
+    tile_count = shell_count // per + 1
+    blocks = sources
+
+    def body(*refs):
+        sum_shells_body(*refs, shell_size=shell_size, depth=depth, blocks=blocks)
+
+    return pl.pallas_call(
+        body,
+        out_shape=jax.ShapeDtypeStruct((8, blocks // 4, rows, lanes), jnp.bfloat16),
+        in_specs=[
+            pl.BlockSpec(memory_space=pltpu.SMEM),
+            pl.BlockSpec(memory_space=pltpu.SMEM),
+            pl.BlockSpec(memory_space=pltpu.VMEM),
+        ],
+        out_specs=pl.BlockSpec(memory_space=pltpu.VMEM),
+        scratch_shapes=[pltpu.VMEM((tile_count, rows, lanes), jnp.float32)],
+        compiler_params=pltpu.CompilerParams(vmem_limit_bytes=32 * 1024 * 1024),
+        cost_estimate=pl.CostEstimate(flops=10**7, bytes_accessed=4 * 10**6, transcendentals=0),
+        name="sum_shells",
+    )(nu, at, got)
+
+
+def transform_body(*refs, chunk):
+    half_ref, out_ref = refs[0], refs[-1]
+    panels = refs[1:-1]
+    groups, blocks, rows, lanes = half_ref.shape
+    depth, columns = panels[0].shape
+    for start in range(0, columns, chunk):
+        total = None
+        for block, panel in enumerate(panels):
+            half = half_ref[:, block].reshape(groups * rows, lanes)[:, :depth]
+            term = jnp.dot(half, panel[:, start : start + chunk], preferred_element_type=jnp.float32)
+            total = term if total is None else total + term
+        out_ref[:, :, start : start + chunk] = total.astype(out_ref.dtype).reshape(groups, rows, chunk)
+
+
+def transform(half, panels, chunk):
+    groups, blocks, rows, lanes = half.shape
+    depth, columns = panels[0].shape
+
+    def body(*refs):
+        transform_body(*refs, chunk=chunk)
+
+    return pl.pallas_call(
+        body,
+        out_shape=jax.ShapeDtypeStruct((groups, rows, columns), jnp.bfloat16),
+        in_specs=[pl.BlockSpec(memory_space=pltpu.VMEM)] * (1 + len(panels)),
+        out_specs=pl.BlockSpec(memory_space=pltpu.VMEM),
+        compiler_params=pltpu.CompilerParams(vmem_limit_bytes=32 * 1024 * 1024),
+        cost_estimate=pl.CostEstimate(
+            flops=2 * groups * rows * blocks * depth * columns, bytes_accessed=6 * 10**6, transcendentals=0
+        ),
+        name="second_quarter",
+    )(half, *panels)
+
+
+def on_device(tiles, occ_coef, vir_coef, shell_pairs, live_flags):
+    slot_count, shell_size, unused_dim, ket_cols = tiles.shape
+    basis_count, occ_count = occ_coef.shape
+    shell_count = basis_count // shell_size
+    depth, vir_count = vir_coef.shape
+    device_count = lax.axis_size(AXES)
+    device_index = lax.axis_index(AXES)
+    core, far, col = lax.axis_index(CORE), lax.axis_index(FAR), lax.axis_index(COL)
+    ket_owned = ket_cols // device_count
+    swap = [(0, 1), (1, 0)]
+
+    width = vir_count // 2
+    keep = lax.dynamic_slice_in_dim(vir_coef, core * width, width, 1)
+    give = lax.dynamic_slice_in_dim(vir_coef, (1 - core) * width, width, 1)
+    near = [keep, lax.ppermute(give, CORE, swap)]
+    beside = [lax.ppermute(panel, COL, swap) for panel in near]
+    away = [lax.ppermute(panel, FAR, swap) for panel in near]
+
+    flags = live_flags.reshape(device_count, slot_count)
+    rank = jnp.cumsum(flags, axis=1) - 1
+    chosen = (rank[:, None, :] == jnp.arange(LIVE)[None, :, None]) & (flags[:, None, :] == 1)
+    nu_table = shell_pairs[1].reshape(device_count, 1, slot_count)
+    nu = jnp.where(jnp.any(chosen, axis=2), jnp.sum(jnp.where(chosen, nu_table, 0), axis=2), shell_count)
+    me = jnp.reshape(device_index, (1,)).astype(jnp.int32)
+    quarter = first_quarter(me, live_flags, shell_pairs, occ_coef.T, tiles, device_count)
+    quarter, near[1], beside[0], away[0] = lax.optimization_barrier((quarter, near[1], beside[0], away[0]))
+    got = lax.all_to_all(quarter, AXES, split_axis=0, concat_axis=0, tiled=True)
+    corner = [lax.ppermute(away[0], COL, swap)]
+    got, beside[1], away[1], corner[0] = lax.optimization_barrier((got, beside[1], away[1], corner[0]))
+    corner.append(lax.ppermute(away[1], COL, swap))
+
+    half = sum_shells(nu.reshape(-1), jnp.stack([far, col]), got, shell_size, shell_count, depth)
+    half = lax.all_to_all(half, (NEAR, ROW, CORE), split_axis=0, concat_axis=0, tiled=True)
+    part = transform(half, near + beside + away + corner, 512)
+    part = lax.all_to_all(part, (NEAR, ROW, CORE), split_axis=0, concat_axis=0, tiled=True)
+    part = part.reshape(4, 2, ket_owned * occ_count, width).astype(jnp.float32).sum(axis=0)
+    return part.transpose(1, 0, 2).reshape(ket_owned, occ_count, vir_count).astype(jnp.bfloat16)
+
+
 def solution(mesh):
+    shape = dict(mesh.shape)
     in_specs = (
         P(("pair", "coef"), None, None, None),
         P("coef", "groups"),
@@ -52,6 +267,10 @@
         P(),
     )
     out_specs = P("pair", "groups", "coef")
-    return jax.shard_map(
-        on_device, mesh=mesh, in_specs=in_specs, out_specs=out_specs, check_vma=False
-    )
+    body = plain
+    if shape["pair"] == 32 and shape["coef"] == 1 and shape["groups"] == 1:
+        mesh = Mesh(mesh.devices.reshape(2, 2, 2, 2, 2), AXES)
+        in_specs = (P(AXES), P(), P(AXES), P(), P())
+        out_specs = P(AXES)
+        body = on_device
+    return jax.shard_map(body, mesh=mesh, in_specs=in_specs, out_specs=out_specs, check_vma=False)

time: 300 us -> 126 us (0.42)
  blocking collectives: 191 us -> 22.9 us
  waiting for transfers between devices: 0.73 us -> 53.8 us
  local copies, waits for them, and re-layouts: 57.1 us -> 8.37 us
  matrix products: 36.9 us -> 0 us
  starting transfers between devices: 0.01 us -> 21.4 us
  Pallas kernels: 0 us -> 18.4 us
  between operations: 13.5 us -> 0.1 us
    all_to_all x1, blocking collectives: 191 us -> 22.9 us  [on_device(): lax.all_to_all(part, (NEAR, ROW, CORE), split_axis=0, concat_axis=0, tile...]
    ppermute x0 -> x7, waiting for transfers between devices: none -> 51.5 us  [the longest x2 41.6 us: on_device(): away = [lax.ppermute(panel, FAR, swap) for panel in near]]
    dot_general x3 -> x0, matrix products: 36.9 us -> none  [the longest x1 13.2 us: on_device(): jnp.einsum('gb,bkis->kigs', selector, received, precision=lax.Precision.H...]
    reshape x6 -> x0, local copies, waits for them, and re-layouts: 28.6 us -> none  [the longest x2 18.1 us: on_device(): quarter = result.reshape(tiles.shape[0], ket_cols, occ_count * shell_size)]
    pallas_call x0 -> x3, Pallas kernels: none -> 18.4 us  [the longest x1 8.98 us: first_quarter(): pl.pallas_call(body, out_shape=jax.ShapeDtypeStruct(shape, jnp.bfloat16),...]
    unnamed x1 -> x12, local copies, waits for them, and re-layouts: 23.3 us -> 5.13 us
    ppermute x0 -> x7, starting transfers between devices: none -> 12 us  [the longest x2 6.03 us: on_device(): away = [lax.ppermute(panel, FAR, swap) for panel in near]]
    all_to_all x0 -> x2, starting transfers between devices: none -> 9.36 us  [the longest x1 5.8 us: on_device(): got = lax.all_to_all(quarter, AXES, split_axis=0, concat_axis=0, tiled=True)]
  transfers between devices with their start and end apart: 1 -> 9, of which waited for: 0 -> 4; matrix products, arithmetic and copies ran while one was open for 20% -> 1% of each run, Pallas kernels for 0% -> 7%
where the time goes in v1:
time: 126 us; the launch traced here: 125 us
  waiting for transfers between devices  53.8 us (43%)
  blocking collectives  22.9 us (18%)
  starting transfers between devices  21.4 us (17%)
  Pallas kernels  18.4 us (15%)
  local copies, waits for them, and re-layouts  8.37 us (7%)
    ppermute x2, waiting for transfers between devices, on_device(): away = [lax.ppermute(panel, FAR, swap) for panel in near]  41.6 us
    all_to_all x1, blocking collectives, on_device(): lax.all_to_all(part, (NEAR, ROW, CORE), split_axis=0, concat_axis=0, tile...  22.9 us
    ppermute x1, waiting for transfers between devices, on_device(): corner.append(lax.ppermute(away[1], COL, swap))  9.89 us
    pallas_call x1, Pallas kernels, first_quarter(): pl.pallas_call(body, out_shape=jax.ShapeDtypeStruct(shape, jnp.bfloat16),...  8.98 us
    ppermute x2, starting transfers between devices, on_device(): away = [lax.ppermute(panel, FAR, swap) for panel in near]  6.03 us
    all_to_all x1, starting transfers between devices, on_device(): got = lax.all_to_all(quarter, AXES, split_axis=0, concat_axis=0, tiled=True)  5.8 us
    unnamed x12, local copies, waits for them, and re-layouts  5.13 us
    pallas_call x1, Pallas kernels, sum_shells(): pl.pallas_call(body, out_shape=jax.ShapeDtypeStruct((8, blocks // 4, rows...  5 us
  transfers between devices with their start and end apart: 9, of which 4 were waited for; matrix products, arithmetic and copies ran while one was open for 1% of the time, Pallas kernels for 7%

profile of v1, /device:TPU:0, one launch (start us, length us, event | category | flops | bytes accessed | tf_op | source)
XLA Modules:
  0.0 125.4 jit_solution(18195995443200138022)
XLA Ops:
  0.0 0.0 copy-start.3
  0.0 0.0 copy-start.2
  0.0 0.0 copy-start.1
  0.0 1.2 constant_dynamic-slice_fusion
  1.2 0.5 collective-permute-start
  1.8 3.7 %collective-permute-start.2 = (bf16[124,1536]{1,0:T(8,128)(2,1)S(1)}, bf16[124,1536]{1,0:T(8,128)(2,1)S(1)}, u32[]{:S(2)}, u32[]{:S(2)}) collective-permute-start(bf16[124,1536]{1,0:T(8,128)(2,1)S(1)} %get-tuple-element.21.refs_1_), channel_id=1, source_target_pairs={{0,16},{16,0},{1,17},{17,1},{2,18},{18,2},{3,19},{19,3},{4,20},{20... | collective-permute-start | bytes 1142792 | tf_op jit(solution)/shard_map/ppermute | solution.py:237
  5.4 1.5 %collective-permute-start.1 = (bf16[124,1536]{1,0:T(8,128)(2,1)S(1)}, bf16[124,1536]{1,0:T(8,128)(2,1)S(1)}, u32[]{:S(2)}, u32[]{:S(2)}) collective-permute-start(bf16[124,1536]{1,0:T(8,128)(2,1)S(1)} %get-tuple-element.21.refs_1_), channel_id=1, source_target_pairs={{0,2},{2,0},{1,3},{3,1},{4,6},{6,4},{5,7},{7,5},{8,10},{10,8},{9,1... | collective-permute-start | bytes 1142792 | tf_op jit(solution)/shard_map/ppermute | solution.py:236
  6.9 0.0 copy-done.3
  6.9 0.0 copy-done.2
  6.9 0.0 copy-done.1
  6.9 0.0 copy-start
  6.9 3.4 %copy-done = bf16[8,64,64,64]{3,2,1,0:T(8,128)(2,1)S(1)} copy-done((bf16[8,64,64,64]{3,2,1,0:T(8,128)(2,1)S(1)}, bf16[8,64,64,64]{3,2,1,0:T(8,128)(2,1)}, u32[]{:S(2)}) %copy-start) | copy-done | bytes 4194328
  10.3 9.0 %first_quarter.1 = bf16[32,2,64,128]{3,2,1,0:T(8,128)(2,1)} custom-call(s32[1]{0:T(128)} %bitcast.2.refs_0_, s32[256]{0:T(256)S(1)} %copy-done.3, s32[2,256]{1,0:T(2,128)S(1)} %copy-done.2, bf16[32,3968]{1,0:T(8,128)(2,1)S(1)} %bitcast.6, bf16[8,64,64,64]{3,2,1,0:T(8,128)(2,1)S(1)} %copy-done), custom_call_target="tpu_custom_call" | custom-call | flops 1000000000 | bytes 6000000 | tf_op jit(solution)/shard_map/first_quarter/pallas_call | solution.py:106
  19.3 0.0 collective-permute-done.refs_2_
  19.3 4.3 %collective-permute-done.2.refs_5_ = bf16[124,1536]{1,0:T(8,128)(2,1)S(1)} collective-permute-done((bf16[124,1536]{1,0:T(8,128)(2,1)S(1)}, bf16[124,1536]{1,0:T(8,128)(2,1)S(1)}, u32[]{:S(2)}, u32[]{:S(2)}) %collective-permute-start.2) | collective-permute-done | bytes 380960 | tf_op jit(solution)/shard_map/ppermute | solution.py:237
  23.6 0.0 collective-permute-done.1.refs_3_
  23.6 5.8 %all-to-all-start = ((bf16[32,2,64,128]{3,2,1,0:T(8,128)(2,1)}), bf16[32,2,64,128]{3,2,1,0:T(8,128)(2,1)S(1)}, u32[]{:S(2)}, u32[]{:S(2)}) async-start(bf16[32,2,64,128]{3,2,1,0:T(8,128)(2,1)} %first_quarter.1), calls=%async_computation | async-start | bytes 2097152 | tf_op jit(solution)/shard_map/all_to_all | solution.py:247
  29.4 0.1 reduce_window_sum.13
  29.5 0.1 broadcast_in_dim.20
  29.6 0.1 copy.9
  29.6 0.2 reduce_window_sum.14
  29.8 0.1 copy.8
  29.9 0.1 copy.7
  30.0 1.8 %collective-permute-start.5 = (bf16[124,1536]{1,0:T(8,128)(2,1)S(1)}, bf16[124,1536]{1,0:T(8,128)(2,1)S(1)}, u32[]{:S(2)}, u32[]{:S(2)}) collective-permute-start(bf16[124,1536]{1,0:T(8,128)(2,1)S(1)} %collective-permute-done.2.refs_5_), channel_id=1, source_target_pairs={{0,2},{2,0},{1,3},{3,1},{4,6},{6,4},{5,7},{7,5},{8,10},{10,8},{9,1... | collective-permute-start | bytes 1142792 | tf_op jit(solution)/shard_map/ppermute | solution.py:248
  31.8 2.4 %collective-permute-start.4 = (bf16[124,1536]{1,0:T(8,128)(2,1)S(1)}, bf16[124,1536]{1,0:T(8,128)(2,1)S(1)}, u32[]{:S(2)}, u32[]{:S(2)}) collective-permute-start(bf16[124,1536]{1,0:T(8,128)(2,1)S(1)} %collective-permute-done.refs_2_), channel_id=1, source_target_pairs={{0,16},{16,0},{1,17},{17,1},{2,18},{18,2},{3,19},{19,3},{4,20},{20... | collective-permute-start | bytes 1142792 | tf_op jit(solution)/shard_map/ppermute | solution.py:237
  34.2 0.6 collective-permute-start.3
  34.8 0.1 copy.10
  34.9 0.1 select_n.20.refs_0_
  35.0 0.1 pad_add_fusion.refs_1_
  35.1 37.4 %collective-permute-done.4.refs_6_ = bf16[124,1536]{1,0:T(8,128)(2,1)S(1)} collective-permute-done((bf16[124,1536]{1,0:T(8,128)(2,1)S(1)}, bf16[124,1536]{1,0:T(8,128)(2,1)S(1)}, u32[]{:S(2)}, u32[]{:S(2)}) %collective-permute-start.4) | collective-permute-done | bytes 380960 | tf_op jit(solution)/shard_map/ppermute | solution.py:237
  72.5 0.0 collective-permute-done.3.refs_4_
  72.5 0.0 collective-permute-done.5.refs_7_
  72.5 0.0 all-to-all-done.refs_2_
  72.5 5.0 %sum_shells.1 = bf16[8,8,64,128]{3,2,1,0:T(8,128)(2,1)} custom-call(s32[128]{0:T(128)S(1)} %select_n.20.refs_0_, s32[2]{0:T(128)S(1)} %pad_add_fusion.refs_1_, bf16[32,2,64,128]{3,2,1,0:T(8,128)(2,1)S(1)} %all-to-all-done.refs_2_), custom_call_target="tpu_custom_call" | custom-call | flops 10000000 | bytes 4000000 | tf_op jit(solution)/shard_map/sum_shells/pallas_call | solution.py:171
  77.5 3.6 %all-to-all-start.1 = ((bf16[8,8,64,128]{3,2,1,0:T(8,128)(2,1)}), bf16[8,8,64,128]{3,2,1,0:T(8,128)(2,1)S(1)}, u32[]{:S(2)}, u32[]{:S(2)}) async-start(bf16[8,8,64,128]{3,2,1,0:T(8,128)(2,1)} %sum_shells.1), calls=%async_computation.1 | async-start | bytes 2097152 | tf_op jit(solution)/shard_map/all_to_all | solution.py:253
  81.0 1.5 %collective-permute-start.6 = (bf16[124,1536]{1,0:T(8,128)(2,1)S(1)}, bf16[124,1536]{1,0:T(8,128)(2,1)S(1)}, u32[]{:S(2)}, u32[]{:S(2)}) collective-permute-start(bf16[124,1536]{1,0:T(8,128)(2,1)S(1)} %collective-permute-done.4.refs_6_), channel_id=1, source_target_pairs={{0,2},{2,0},{1,3},{3,1},{4,6},{6,4},{5,7},{7,5},{8,10},{10,8},{9,1... | collective-permute-start | bytes 1142792 | tf_op jit(solution)/shard_map/ppermute | solution.py:250
  82.6 9.9 %collective-permute-done.6.refs_8_ = bf16[124,1536]{1,0:T(8,128)(2,1)S(1)} collective-permute-done((bf16[124,1536]{1,0:T(8,128)(2,1)S(1)}, bf16[124,1536]{1,0:T(8,128)(2,1)S(1)}, u32[]{:S(2)}, u32[]{:S(2)}) %collective-permute-start.6) | collective-permute-done | bytes 380960 | tf_op jit(solution)/shard_map/ppermute | solution.py:250
  92.5 0.0 copy-start.4
  92.5 0.7 copy-done.4
  93.2 2.2 %all-to-all-done.1.refs_0_ = bf16[8,8,64,128]{3,2,1,0:T(8,128)(2,1)S(1)} async-done(((bf16[8,8,64,128]{3,2,1,0:T(8,128)(2,1)}), bf16[8,8,64,128]{3,2,1,0:T(8,128)(2,1)S(1)}, u32[]{:S(2)}, u32[]{:S(2)}) %all-to-all-start.1) | async-done | bytes 1048608 | tf_op jit(solution)/shard_map/all_to_all | solution.py:253
  95.4 0.0 copy-start.5
  95.4 1.0 copy-done.5
  96.4 4.4 %second_quarter.1 = bf16[8,64,1536]{2,1,0:T(8,128)(2,1)S(1)} custom-call(bf16[8,8,64,128]{3,2,1,0:T(8,128)(2,1)S(1)} %all-to-all-done.1.refs_0_, bf16[124,1536]{1,0:T(8,128)(2,1)S(1)} %get-tuple-element.21.refs_1_, bf16[124,1536]{1,0:T(8,128)(2,1)S(1)} %collective-permute-done.refs_2_, bf16[124,1536]{1,0:T(8,128)(2,1)S(1)} %collective-permute-done.1.refs_3_, ...), custom_call_target="tpu_custom_call" | custom-call | flops 1560281088 | bytes 6000000 | tf_op jit(solution)/shard_map/second_quarter/pallas_call | solution.py:208
  100.8 22.9 %all_to_all.15 = bf16[8,64,1536]{2,1,0:T(8,128)(2,1)S(1)} all-to-all(bf16[8,64,1536]{2,1,0:T(8,128)(2,1)S(1)} %second_quarter.1), channel_id=1, replica_groups=mesh['far'=2,'near'=2,'row'=2,'col'=2,'core'=2] {'near','row','core'}, dimensions={0} | all-to-all | bytes 3145728 | tf_op jit(solution)/shard_map/all_to_all | solution.py:255
  123.7 0.3 reduce
  123.9 0.4 copy.11
  124.3 1.0 convert_element_type.19
  (6 shorter events, 0.1 us)
Async XLA Ops:
  0.0 6.9 %copy-start.3 = (s32[256]{0:T(256)S(1)}, s32[256]{0:T(256)}, u32[]{:S(2)}) copy-start(s32[256]{0:T(256)} %refs_1_.1) | copy-start | bytes 3076
  0.0 6.9 %copy-start.2 = (s32[2,256]{1,0:T(2,128)S(1)}, s32[2,256]{1,0:T(2,128)}, u32[]{:S(2)}) copy-start(s32[2,256]{1,0:T(2,128)} %refs_2_.1) | copy-start | bytes 6148
  0.0 6.9 %copy-start.1 = (bf16[3968,32]{0,1:T(8,128)(2,1)S(1)}, bf16[3968,32]{0,1:T(8,128)(2,1)}, u32[]{:S(2)}) copy-start(bf16[3968,32]{0,1:T(8,128)(2,1)} %param.6) | copy-start | bytes 761860
  1.2 18.1 %collective-permute-start = (bf16[124,1536]{1,0:T(8,128)(2,1)S(1)}, bf16[124,1536]{1,0:T(8,128)(2,1)S(1)}, u32[]{:S(2)}, u32[]{:S(2)}) collective-permute-start(bf16[124,1536]{1,0:T(8,128)(2,1)S(1)} %get-tuple-element.22), channel_id=1, source_target_pairs={{0,1},{1,0},{2,3},{3,2},{4,5},{5,4},{6,7},{7,6},{8,9},{9,8},{10,11... | collective-permute-start | bytes 1142792 | tf_op jit(solution)/shard_map/ppermute | solution.py:235
  1.8 21.8 %collective-permute-start.2 = (bf16[124,1536]{1,0:T(8,128)(2,1)S(1)}, bf16[124,1536]{1,0:T(8,128)(2,1)S(1)}, u32[]{:S(2)}, u32[]{:S(2)}) collective-permute-start(bf16[124,1536]{1,0:T(8,128)(2,1)S(1)} %get-tuple-element.21.refs_1_), channel_id=1, source_target_pairs={{0,16},{16,0},{1,17},{17,1},{2,18},{18,2},{3,19},{19,3},{4,20},{20... | collective-permute-start | bytes 1142792 | tf_op jit(solution)/shard_map/ppermute | solution.py:237
  5.4 18.1 %collective-permute-start.1 = (bf16[124,1536]{1,0:T(8,128)(2,1)S(1)}, bf16[124,1536]{1,0:T(8,128)(2,1)S(1)}, u32[]{:S(2)}, u32[]{:S(2)}) collective-permute-start(bf16[124,1536]{1,0:T(8,128)(2,1)S(1)} %get-tuple-element.21.refs_1_), channel_id=1, source_target_pairs={{0,2},{2,0},{1,3},{3,1},{4,6},{6,4},{5,7},{7,5},{8,10},{10,8},{9,1... | collective-permute-start | bytes 1142792 | tf_op jit(solution)/shard_map/ppermute | solution.py:236
  6.9 3.4 %copy-start = (bf16[8,64,64,64]{3,2,1,0:T(8,128)(2,1)S(1)}, bf16[8,64,64,64]{3,2,1,0:T(8,128)(2,1)}, u32[]{:S(2)}) copy-start(bf16[8,64,64,64]{3,2,1,0:T(8,128)(2,1)} %refs_4_.1) | copy-start | bytes 12582916
  23.6 48.9 %all-to-all-start = ((bf16[32,2,64,128]{3,2,1,0:T(8,128)(2,1)}), bf16[32,2,64,128]{3,2,1,0:T(8,128)(2,1)S(1)}, u32[]{:S(2)}, u32[]{:S(2)}) async-start(bf16[32,2,64,128]{3,2,1,0:T(8,128)(2,1)} %first_quarter.1), calls=%async_computation | async-start | bytes 2097152 | tf_op jit(solution)/shard_map/all_to_all | solution.py:247
  30.0 42.5 %collective-permute-start.5 = (bf16[124,1536]{1,0:T(8,128)(2,1)S(1)}, bf16[124,1536]{1,0:T(8,128)(2,1)S(1)}, u32[]{:S(2)}, u32[]{:S(2)}) collective-permute-start(bf16[124,1536]{1,0:T(8,128)(2,1)S(1)} %collective-permute-done.2.refs_5_), channel_id=1, source_target_pairs={{0,2},{2,0},{1,3},{3,1},{4,6},{6,4},{5,7},{7,5},{8,10},{10,8},{9,1... | collective-permute-start | bytes 1142792 | tf_op jit(solution)/shard_map/ppermute | solution.py:248
  31.8 40.6 %collective-permute-start.4 = (bf16[124,1536]{1,0:T(8,128)(2,1)S(1)}, bf16[124,1536]{1,0:T(8,128)(2,1)S(1)}, u32[]{:S(2)}, u32[]{:S(2)}) collective-permute-start(bf16[124,1536]{1,0:T(8,128)(2,1)S(1)} %collective-permute-done.refs_2_), channel_id=1, source_target_pairs={{0,16},{16,0},{1,17},{17,1},{2,18},{18,2},{3,19},{19,3},{4,20},{20... | collective-permute-start | bytes 1142792 | tf_op jit(solution)/shard_map/ppermute | solution.py:237
  34.2 38.3 %collective-permute-start.3 = (bf16[124,1536]{1,0:T(8,128)(2,1)S(1)}, bf16[124,1536]{1,0:T(8,128)(2,1)}, u32[]{:S(2)}, u32[]{:S(2)}) collective-permute-start(bf16[124,1536]{1,0:T(8,128)(2,1)S(1)} %collective-permute-done.refs_2_), channel_id=1, source_target_pairs={{0,2},{2,0},{1,3},{3,1},{4,6},{6,4},{5,7},{7,5},{8,10},{10,8},{9,1... | collective-permute-start | bytes 1142792 | tf_op jit(solution)/shard_map/ppermute | solution.py:236
  77.5 17.9 %all-to-all-start.1 = ((bf16[8,8,64,128]{3,2,1,0:T(8,128)(2,1)}), bf16[8,8,64,128]{3,2,1,0:T(8,128)(2,1)S(1)}, u32[]{:S(2)}, u32[]{:S(2)}) async-start(bf16[8,8,64,128]{3,2,1,0:T(8,128)(2,1)} %sum_shells.1), calls=%async_computation.1 | async-start | bytes 2097152 | tf_op jit(solution)/shard_map/all_to_all | solution.py:253
  81.0 11.4 %collective-permute-start.6 = (bf16[124,1536]{1,0:T(8,128)(2,1)S(1)}, bf16[124,1536]{1,0:T(8,128)(2,1)S(1)}, u32[]{:S(2)}, u32[]{:S(2)}) collective-permute-start(bf16[124,1536]{1,0:T(8,128)(2,1)S(1)} %collective-permute-done.4.refs_6_), channel_id=1, source_target_pairs={{0,2},{2,0},{1,3},{3,1},{4,6},{6,4},{5,7},{7,5},{8,10},{10,8},{9,1... | collective-permute-start | bytes 1142792 | tf_op jit(solution)/shard_map/ppermute | solution.py:250
  92.5 0.7 copy-start.4
  95.4 1.0 copy-start.5

commit v2 on v1

--- a/solution.py
+++ b/solution.py
@@ -47,6 +47,21 @@
         preferred_element_type=jnp.float32,
     )
     return result.reshape(ket_owned, occ_count, vir_coef.shape[1]).astype(jnp.bfloat16)
+
+
+def shell_list_body(nu_ref, out_ref):
+    out_ref[...] = nu_ref[...]
+
+
+def shell_list(nu):
+    return pl.pallas_call(
+        shell_list_body,
+        out_shape=jax.ShapeDtypeStruct(nu.shape, nu.dtype),
+        in_specs=[pl.BlockSpec(memory_space=pltpu.VMEM)],
+        out_specs=pl.BlockSpec(memory_space=pltpu.VMEM),
+        cost_estimate=pl.CostEstimate(flops=10**11, bytes_accessed=10**6, transcendentals=0),
+        name="shell_list",
+    )(nu)
 
 
 def first_quarter_body(me_ref, flag_ref, pair_ref, occ_ref, tiles_ref, out_ref, held, turned, wide, sem, *, slots):
@@ -115,13 +130,14 @@
             pltpu.VMEM((ket_cols * occ_count, 2 * shell_size), jnp.float32),
             pltpu.SemaphoreType.DMA((LIVE,)),
         ],
-        compiler_params=pltpu.CompilerParams(vmem_limit_bytes=32 * 1024 * 1024),
+        compiler_params=pltpu.CompilerParams(vmem_limit_bytes=60 * 1024 * 1024),
         cost_estimate=pl.CostEstimate(flops=10**9, bytes_accessed=6 * 10**6, transcendentals=0),
         name="first_quarter",
     )(me, flags, pairs, occ, tiles)
 
 
-def sum_shells_body(nu_ref, at_ref, got_ref, out_ref, acc_ref, *, shell_size, depth, blocks):
+def sum_shells_body(nu_ref, at_ref, got_ref, *refs, shell_size, depth):
+    outs, acc_ref = refs[:-1], refs[-1]
     tile_count, rows, lanes = acc_ref.shape
     per = lanes // shell_size
     sources, groups = got_ref.shape[0], got_ref.shape[1]
@@ -142,41 +158,36 @@
         return carry
 
     lax.fori_loop(0, sources, add, 0)
-    far, col = at_ref[0], at_ref[1]
-    for block in range(blocks):
-        first = block * depth
-        tile, shift = first // lanes, first % lanes
-        turn = (lanes - shift) % lanes
-        value = acc_ref[tile]
-        if turn:
-            value = pltpu.roll(value, turn, 1)
-            if shift + depth > lanes:
-                value = jnp.where(lane < turn, value, pltpu.roll(acc_ref[tile + 1], turn, 1))
-        value = jnp.where(lane < depth, value, 0.0).astype(out_ref.dtype)
-        bits = [(block >> b) & 1 for b in (4, 3, 2, 1, 0)]
-        spot = 4 * jnp.bitwise_xor(far, bits[0]) + 2 * jnp.bitwise_xor(col, bits[3])
-        for core in range(2):
-            out_ref[4 * bits[1] + 2 * bits[2] + core, spot + (bits[4] ^ core)] = value
+    step = lanes - depth
+    for piece, out_ref in enumerate(outs):
+        for spot in range(out_ref.shape[0]):
+            flips = (piece >> 1, spot >> 2, (spot >> 1) & 1, spot & 1, piece & 1)
+            block = jnp.int32(0)
+            for axis, flip in enumerate(flips):
+                block = 2 * block + jnp.bitwise_xor(at_ref[axis], flip)
+            turn = block * step
+            before = pltpu.roll(acc_ref[jnp.maximum(block - 1, 0)], turn, 1)
+            after = pltpu.roll(acc_ref[block], turn, 1)
+            value = jnp.where(lane < turn, before, after)
+            out_ref[spot] = jnp.where(lane < depth, value, 0.0).astype(out_ref.dtype)
 
 
 def sum_shells(nu, at, got, shell_size, shell_count, depth):
     sources, groups, rows, lanes = got.shape
-    per = lanes // shell_size
-    tile_count = shell_count // per + 1
-    blocks = sources
+    tile_count = shell_count // (lanes // shell_size) + 1
 
     def body(*refs):
-        sum_shells_body(*refs, shell_size=shell_size, depth=depth, blocks=blocks)
+        sum_shells_body(*refs, shell_size=shell_size, depth=depth)
 
     return pl.pallas_call(
         body,
-        out_shape=jax.ShapeDtypeStruct((8, blocks // 4, rows, lanes), jnp.bfloat16),
+        out_shape=[jax.ShapeDtypeStruct((sources // 4, rows, lanes), jnp.bfloat16)] * 4,
         in_specs=[
             pl.BlockSpec(memory_space=pltpu.SMEM),
             pl.BlockSpec(memory_space=pltpu.SMEM),
             pl.BlockSpec(memory_space=pltpu.VMEM),
         ],
-        out_specs=pl.BlockSpec(memory_space=pltpu.VMEM),
+        out_specs=[pl.BlockSpec(memory_space=pltpu.VMEM)] * 4,
         scratch_shapes=[pltpu.VMEM((tile_count, rows, lanes), jnp.float32)],
         compiler_params=pltpu.CompilerParams(vmem_limit_bytes=32 * 1024 * 1024),
         cost_estimate=pl.CostEstimate(flops=10**7, bytes_accessed=4 * 10**6, transcendentals=0),
@@ -184,38 +195,56 @@
     )(nu, at, got)
 
 
-def transform_body(*refs, chunk):
-    half_ref, out_ref = refs[0], refs[-1]
-    panels = refs[1:-1]
-    groups, blocks, rows, lanes = half_ref.shape
+def transform_body(*refs, chunk, part, count, pieces):
+    halves, panels = refs[:pieces], refs[pieces : pieces + count]
+    outs, held, sems = refs[pieces + count : -2], refs[-2], refs[-1]
     depth, columns = panels[0].shape
-    for start in range(0, columns, chunk):
+    rows = halves[0].shape[1]
+    copies = [
+        [
+            pltpu.make_async_copy(panel.at[:, pl.ds(start, chunk)], held.at[block, :, pl.ds(start, chunk)], sems.at[step, block])
+            for block, panel in enumerate(panels)
+        ]
+        for step, start in enumerate(range(0, columns, chunk))
+    ]
+    for row in copies:
+        for copy in row:
+            copy.start()
+    for start in range(0, columns, part):
         total = None
-        for block, panel in enumerate(panels):
-            half = half_ref[:, block].reshape(groups * rows, lanes)[:, :depth]
-            term = jnp.dot(half, panel[:, start : start + chunk], preferred_element_type=jnp.float32)
+        for block in range(count):
+            if start % chunk == 0:
+                copies[start // chunk][block].wait()
+            half = jnp.concatenate([half_ref[block] for half_ref in halves], axis=0)[:, :depth]
+            term = jnp.dot(half, held[block, :, start : start + part], preferred_element_type=jnp.float32)
             total = term if total is None else total + term
-        out_ref[:, :, start : start + chunk] = total.astype(out_ref.dtype).reshape(groups, rows, chunk)
-
-
-def transform(half, panels, chunk):
-    groups, blocks, rows, lanes = half.shape
+        for piece, out_ref in enumerate(outs):
+            out_ref[:, start : start + part] = total[piece * rows : (piece + 1) * rows].astype(out_ref.dtype)
+
+
+def transform(halves, panels, dtypes, chunk, part):
+    blocks, rows, lanes = halves[0].shape
     depth, columns = panels[0].shape
+    pieces = len(halves)
 
     def body(*refs):
-        transform_body(*refs, chunk=chunk)
+        transform_body(*refs, chunk=chunk, part=part, count=blocks, pieces=pieces)
 
     return pl.pallas_call(
         body,
-        out_shape=jax.ShapeDtypeStruct((groups, rows, columns), jnp.bfloat16),
-        in_specs=[pl.BlockSpec(memory_space=pltpu.VMEM)] * (1 + len(panels)),
-        out_specs=pl.BlockSpec(memory_space=pltpu.VMEM),
-        compiler_params=pltpu.CompilerParams(vmem_limit_bytes=32 * 1024 * 1024),
+        out_shape=[jax.ShapeDtypeStruct((rows, columns), dtype) for dtype in dtypes],
+        in_specs=[pl.BlockSpec(memory_space=pltpu.VMEM)] * pieces + [pl.BlockSpec(memory_space=pl.ANY)] * blocks,
+        out_specs=[pl.BlockSpec(memory_space=pltpu.VMEM)] * pieces,
+        scratch_shapes=[
+            pltpu.VMEM((blocks, depth, columns), jnp.bfloat16),
+            pltpu.SemaphoreType.DMA((columns // chunk, blocks)),
+        ],
+        compiler_params=pltpu.CompilerParams(vmem_limit_bytes=60 * 1024 * 1024),
         cost_estimate=pl.CostEstimate(
-            flops=2 * groups * rows * blocks * depth * columns, bytes_accessed=6 * 10**6, transcendentals=0
+            flops=2 * pieces * rows * blocks * depth * columns, bytes_accessed=8 * 10**6, transcendentals=0
         ),
         name="second_quarter",
-    )(half, *panels)
+    )(*halves, *panels)
 
 
 def on_device(tiles, occ_coef, vir_coef, shell_pairs, live_flags):
@@ -225,16 +254,13 @@
     depth, vir_count = vir_coef.shape
     device_count = lax.axis_size(AXES)
     device_index = lax.axis_index(AXES)
-    core, far, col = lax.axis_index(CORE), lax.axis_index(FAR), lax.axis_index(COL)
     ket_owned = ket_cols // device_count
     swap = [(0, 1), (1, 0)]
 
-    width = vir_count // 2
-    keep = lax.dynamic_slice_in_dim(vir_coef, core * width, width, 1)
-    give = lax.dynamic_slice_in_dim(vir_coef, (1 - core) * width, width, 1)
-    near = [keep, lax.ppermute(give, CORE, swap)]
-    beside = [lax.ppermute(panel, COL, swap) for panel in near]
-    away = [lax.ppermute(panel, FAR, swap) for panel in near]
+    diagonal = [(i, 3 - i) for i in range(4)]
+    by_near = lax.ppermute(vir_coef, NEAR, swap)
+    by_row = lax.ppermute(vir_coef, ROW, swap)
+    by_col = lax.ppermute(vir_coef, COL, swap)
 
     flags = live_flags.reshape(device_count, slot_count)
     rank = jnp.cumsum(flags, axis=1) - 1
@@ -243,18 +269,31 @@
     nu = jnp.where(jnp.any(chosen, axis=2), jnp.sum(jnp.where(chosen, nu_table, 0), axis=2), shell_count)
     me = jnp.reshape(device_index, (1,)).astype(jnp.int32)
     quarter = first_quarter(me, live_flags, shell_pairs, occ_coef.T, tiles, device_count)
-    quarter, near[1], beside[0], away[0] = lax.optimization_barrier((quarter, near[1], beside[0], away[0]))
+    quarter, by_near, by_row, by_col = lax.optimization_barrier((quarter, by_near, by_row, by_col))
     got = lax.all_to_all(quarter, AXES, split_axis=0, concat_axis=0, tiled=True)
-    corner = [lax.ppermute(away[0], COL, swap)]
-    got, beside[1], away[1], corner[0] = lax.optimization_barrier((got, beside[1], away[1], corner[0]))
-    corner.append(lax.ppermute(away[1], COL, swap))
-
-    half = sum_shells(nu.reshape(-1), jnp.stack([far, col]), got, shell_size, shell_count, depth)
-    half = lax.all_to_all(half, (NEAR, ROW, CORE), split_axis=0, concat_axis=0, tiled=True)
-    part = transform(half, near + beside + away + corner, 512)
-    part = lax.all_to_all(part, (NEAR, ROW, CORE), split_axis=0, concat_axis=0, tiled=True)
-    part = part.reshape(4, 2, ket_owned * occ_count, width).astype(jnp.float32).sum(axis=0)
-    return part.transpose(1, 0, 2).reshape(ket_owned, occ_count, vir_count).astype(jnp.bfloat16)
+    near_row = lax.ppermute(by_near, ROW, swap)
+    near_col = lax.ppermute(by_col, NEAR, swap)
+    row_col = lax.ppermute(by_row, COL, swap)
+
+    at = jnp.stack([lax.axis_index(axis) for axis in AXES])
+    own, to_core, to_far, to_both = sum_shells(nu.reshape(-1), at, got, shell_size, shell_count, depth)
+    own, near_row = lax.optimization_barrier((own, near_row))
+    all_three = lax.ppermute(near_row, COL, swap)
+    panels = [vir_coef, by_col, by_row, row_col, by_near, near_col, near_row, all_three]
+    from_far = lax.ppermute(to_far, FAR, swap)
+    from_both = lax.ppermute(to_both, (FAR, CORE), diagonal)
+    from_core = lax.ppermute(to_core, CORE, swap)
+    wide, narrow = jnp.float32, jnp.bfloat16
+    own_part, own_peer, far_part, far_peer = transform(
+        [own, from_core, from_far, from_both], panels, [wide, narrow, wide, narrow], 1024, 512
+    )
+    far_peer = lax.ppermute(far_peer, CORE, swap)
+    far_part = (far_part + far_peer.astype(jnp.float32)).astype(jnp.bfloat16)
+    own_peer, far_part = lax.optimization_barrier((own_peer, far_part))
+    taken = lax.ppermute(far_part, FAR, swap)
+    own_peer = lax.ppermute(own_peer, CORE, swap)
+    total = own_part + own_peer.astype(jnp.float32) + taken.astype(jnp.float32)
+    return total.reshape(ket_owned, occ_count, vir_count).astype(jnp.bfloat16)
 
 
 def solution(mesh):

time: 126 us -> 113 us (0.90)
  blocking collectives: 22.9 us -> 0 us
  waiting for transfers between devices: 53.8 us -> 61.7 us
  local copies, waits for them, and re-layouts: 8.37 us -> 2.26 us
  Pallas kernels: 18.4 us -> 22 us
  other arithmetic: 0.57 us -> 3.43 us
  starting transfers between devices: 21.4 us -> 23.1 us
    all_to_all x1 -> x0, blocking collectives: 22.9 us -> none  [on_device(): lax.all_to_all(part, (NEAR, ROW, CORE), split_axis=0, concat_axis=0, tile...]
    all_to_all x1, waiting for transfers between devices: 0.01 us -> 20.6 us  [on_device(): got = lax.all_to_all(quarter, AXES, split_axis=0, concat_axis=0, tiled=True)]
    ppermute x7 -> x13, waiting for transfers between devices: 51.5 us -> 41.2 us  [the longest x1 18.1 us: on_device(): taken = lax.ppermute(far_part, FAR, swap)]
    ppermute x7 -> x13, starting transfers between devices: 12 us -> 19.2 us  [the longest x1 2.97 us: on_device(): by_row = lax.ppermute(vir_coef, ROW, swap)]
    unnamed x12 -> x20, local copies, waits for them, and re-layouts: 5.13 us -> 1.57 us
    all_to_all x1 -> x0, starting transfers between devices: 3.56 us -> none  [on_device(): lax.all_to_all(half, (NEAR, ROW, CORE), split_axis=0, concat_axis=0, tile...]
    convert_element_type x0 -> x2, other arithmetic: none -> 3.2 us  [the longest x1 2 us: on_device(): return total.reshape(ket_owned, occ_count, vir_count).astype(jnp.bfloat16)]
    pallas_call x2, Pallas kernels: 9.38 us -> 11.9 us  [the longest x1 7.85 us: transform(): pl.pallas_call(body, out_shape=[jax.ShapeDtypeStruct((rows, columns), dty...]
  transfers between devices with their start and end apart: 9 -> 14, of which waited for: 4 -> 10; matrix products, arithmetic and copies ran while one was open for 1% -> 1% of each run, Pallas kernels for 7% -> 13%
where the time goes in v2:
time: 113 us
  waiting for transfers between devices  61.7 us (55%)
  starting transfers between devices  23.1 us (20%)
  Pallas kernels  22 us (19%)
  other arithmetic  3.43 us (3%)
  local copies, waits for them, and re-layouts  2.26 us (2%)
    all_to_all x1, waiting for transfers between devices, on_device(): got = lax.all_to_all(quarter, AXES, split_axis=0, concat_axis=0, tiled=True)  20.6 us
    ppermute x1, waiting for transfers between devices, on_device(): taken = lax.ppermute(far_part, FAR, swap)  18.1 us
    pallas_call x1, Pallas kernels, first_quarter(): pl.pallas_call(body, out_shape=jax.ShapeDtypeStruct(shape, jnp.bfloat16),...  10.1 us
    pallas_call x1, Pallas kernels, transform(): pl.pallas_call(body, out_shape=[jax.ShapeDtypeStruct((rows, columns), dty...  7.85 us
    ppermute x1, waiting for transfers between devices, on_device(): from_far = lax.ppermute(to_far, FAR, swap)  7.02 us
    ppermute x1, waiting for transfers between devices, on_device(): by_row = lax.ppermute(vir_coef, ROW, swap)  4.59 us
    pallas_call x1, Pallas kernels, sum_shells(): pl.pallas_call(body, out_shape=[jax.ShapeDtypeStruct((sources // 4, rows,...  4.04 us
    all_to_all x1, starting transfers between devices, on_device(): got = lax.all_to_all(quarter, AXES, split_axis=0, concat_axis=0, tiled=True)  3.88 us
  transfers between devices with their start and end apart: 14, of which 10 were waited for; matrix products, arithmetic and copies ran while one was open for 1% of the time, Pallas kernels for 13%

profile of v2, /device:TPU:0, one launch (start us, length us, event | category | flops | bytes accessed | tf_op | source)
XLA Modules:
  0.0 112.7 jit_solution(2201483654155204710)
XLA Ops:
  0.0 0.0 copy-start.9
  0.0 0.0 copy-start.8
  0.0 3.0 %collective-permute-start.1 = (bf16[124,3072]{1,0:T(8,128)(2,1)}, bf16[124,3072]{1,0:T(8,128)(2,1)S(1)}, u32[]{:S(2)}, u32[]{:S(2)}) collective-permute-start(bf16[124,3072]{1,0:T(8,128)(2,1)} %refs_4_.3), channel_id=1, source_target_pairs={{0,4},{4,0},{1,5},{5,1},{2,6},{6,2},{3,7},{7,3},{8,12},{12,8},{9,1... | collective-permute-start | bytes 2285576 | tf_op jit(solution)/shard_map/ppermute | solution.py:262
  3.0 1.6 %collective-permute-start = (bf16[124,3072]{1,0:T(8,128)(2,1)}, bf16[124,3072]{1,0:T(8,128)(2,1)S(1)}, u32[]{:S(2)}, u32[]{:S(2)}) collective-permute-start(bf16[124,3072]{1,0:T(8,128)(2,1)} %refs_4_.3), channel_id=1, source_target_pairs={{0,8},{8,0},{1,9},{9,1},{2,10},{10,2},{3,11},{11,3},{4,12},{12,4},... | collective-permute-start | bytes 2285576 | tf_op jit(solution)/shard_map/ppermute | solution.py:261
  4.5 1.5 %collective-permute-start.2 = (bf16[124,3072]{1,0:T(8,128)(2,1)}, bf16[124,3072]{1,0:T(8,128)(2,1)S(1)}, u32[]{:S(2)}, u32[]{:S(2)}) collective-permute-start(bf16[124,3072]{1,0:T(8,128)(2,1)} %refs_4_.3), channel_id=1, source_target_pairs={{0,2},{2,0},{1,3},{3,1},{4,6},{6,4},{5,7},{7,5},{8,10},{10,8},{9,1... | collective-permute-start | bytes 2285576 | tf_op jit(solution)/shard_map/ppermute | solution.py:263
  6.0 10.1 %first_quarter.1 = bf16[32,2,64,128]{3,2,1,0:T(8,128)(2,1)} custom-call(s32[1]{0:T(128)} %bitcast.5.refs_0_, s32[256]{0:T(256)} %refs_1_.1, s32[2,256]{1,0:T(2,128)} %refs_2_.1, bf16[32,3968]{1,0:T(8,128)(2,1)} %bitcast.8, bf16[8,64,64,64]{3,2,1,0:T(8,128)(2,1)} %refs_4_.2), custom_call_target="tpu_custom_call" | custom-call | flops 1000000000 | bytes 6000000 | tf_op jit(solution)/shard_map/first_quarter/pallas_call | solution.py:121
  16.1 4.6 %collective-permute-done.1.refs_6_ = bf16[124,3072]{1,0:T(8,128)(2,1)S(1)} collective-permute-done((bf16[124,3072]{1,0:T(8,128)(2,1)}, bf16[124,3072]{1,0:T(8,128)(2,1)S(1)}, u32[]{:S(2)}, u32[]{:S(2)}) %collective-permute-start.1) | collective-permute-done | bytes 761888 | tf_op jit(solution)/shard_map/ppermute | solution.py:262
  20.7 0.0 copy-start.1
  20.7 1.5 %collective-permute-done.refs_8_ = bf16[124,3072]{1,0:T(8,128)(2,1)S(1)} collective-permute-done((bf16[124,3072]{1,0:T(8,128)(2,1)}, bf16[124,3072]{1,0:T(8,128)(2,1)S(1)}, u32[]{:S(2)}, u32[]{:S(2)}) %collective-permute-start) | collective-permute-done | bytes 761888 | tf_op jit(solution)/shard_map/ppermute | solution.py:261
  22.2 0.0 copy-start.2
  22.2 1.3 %collective-permute-done.2.refs_5_ = bf16[124,3072]{1,0:T(8,128)(2,1)S(1)} collective-permute-done((bf16[124,3072]{1,0:T(8,128)(2,1)}, bf16[124,3072]{1,0:T(8,128)(2,1)S(1)}, u32[]{:S(2)}, u32[]{:S(2)}) %collective-permute-start.2) | collective-permute-done | bytes 761888 | tf_op jit(solution)/shard_map/ppermute | solution.py:263
  23.5 0.0 copy-start.3
  23.5 3.9 %all-to-all-start = ((bf16[32,2,64,128]{3,2,1,0:T(8,128)(2,1)}), bf16[32,2,64,128]{3,2,1,0:T(8,128)(2,1)S(1)}, u32[]{:S(2)}, u32[]{:S(2)}) async-start(bf16[32,2,64,128]{3,2,1,0:T(8,128)(2,1)} %first_quarter.1), calls=%async_computation | async-start | bytes 2097152 | tf_op jit(solution)/shard_map/all_to_all | solution.py:273
  27.4 0.0 copy-done.9
  27.4 0.1 reduce_window_sum.13
  27.5 1.8 %collective-permute-start.3 = (bf16[124,3072]{1,0:T(8,128)(2,1)S(1)}, bf16[124,3072]{1,0:T(8,128)(2,1)}, u32[]{:S(2)}, u32[]{:S(2)}) collective-permute-start(bf16[124,3072]{1,0:T(8,128)(2,1)S(1)} %collective-permute-done.refs_8_), channel_id=1, source_target_pairs={{0,4},{4,0},{1,5},{5,1},{2,6},{6,2},{3,7},{7,3},{8,12},{12,8},{9,1... | collective-permute-start | bytes 2285576 | tf_op jit(solution)/shard_map/ppermute | solution.py:274
  29.3 0.0 copy-done.8
  29.3 0.1 broadcast_in_dim.20
  29.4 0.1 copy.8
  29.5 0.1 copy.7
  29.6 0.2 reduce_window_sum.14
  29.7 0.1 copy.6
  29.9 1.5 %collective-permute-start.8 = (bf16[124,3072]{1,0:T(8,128)(2,1)S(1)}, bf16[124,3072]{1,0:T(8,128)(2,1)}, u32[]{:S(2)}, u32[]{:S(2)}) collective-permute-start(bf16[124,3072]{1,0:T(8,128)(2,1)S(1)} %collective-permute-done.2.refs_5_), channel_id=1, source_target_pairs={{0,8},{8,0},{1,9},{9,1},{2,10},{10,2},{3,11},{11,3},{4,12},{12,4},... | collective-permute-start | bytes 2285576 | tf_op jit(solution)/shard_map/ppermute | solution.py:275
  31.4 0.1 copy.9
  31.5 0.1 select_n.14.refs_0_
  31.6 0.1 stack.23.refs_1_
  31.7 1.5 %collective-permute-start.7 = (bf16[124,3072]{1,0:T(8,128)(2,1)S(1)}, bf16[124,3072]{1,0:T(8,128)(2,1)}, u32[]{:S(2)}, u32[]{:S(2)}) collective-permute-start(bf16[124,3072]{1,0:T(8,128)(2,1)S(1)} %collective-permute-done.1.refs_6_), channel_id=1, source_target_pairs={{0,2},{2,0},{1,3},{3,1},{4,6},{6,4},{5,7},{7,5},{8,10},{10,8},{9,1... | collective-permute-start | bytes 2285576 | tf_op jit(solution)/shard_map/ppermute | solution.py:276
  33.2 20.6 %all-to-all-done.refs_2_ = bf16[32,2,64,128]{3,2,1,0:T(8,128)(2,1)S(1)} async-done(((bf16[32,2,64,128]{3,2,1,0:T(8,128)(2,1)}), bf16[32,2,64,128]{3,2,1,0:T(8,128)(2,1)S(1)}, u32[]{:S(2)}, u32[]{:S(2)}) %all-to-all-start) | async-done | bytes 1048608 | tf_op jit(solution)/shard_map/all_to_all | solution.py:273
  53.7 4.0 %sum_shells.1 = (bf16[8,64,128]{2,1,0:T(8,128)(2,1)S(1)}, bf16[8,64,128]{2,1,0:T(8,128)(2,1)S(1)}, bf16[8,64,128]{2,1,0:T(8,128)(2,1)S(1)}, bf16[8,64,128]{2,1,0:T(8,128)(2,1)S(1)}) custom-call(s32[128]{0:T(128)S(1)} %select_n.14.refs_0_, s32[5]{0:T(128)S(1)} %stack.23.refs_1_, bf16[32,2,64,128]{3,2,1,0:T(8,128)(2,1)S(1)} %all-to-all-done.refs_2_), custom_call_target="tpu_custom_call" | custom-call | flops 10000000 | bytes 4000000 | tf_op jit(solution)/shard_map/sum_shells/pallas_call | solution.py:182
  57.8 0.0 copy-start
  57.8 0.6 copy-done
  58.4 0.0 collective-permute-done.3.refs_10_
  58.4 1.5 %collective-permute-start.9 = (bf16[124,3072]{1,0:T(8,128)(2,1)}, bf16[124,3072]{1,0:T(8,128)(2,1)S(1)}, u32[]{:S(2)}, u32[]{:S(2)}) collective-permute-start(bf16[124,3072]{1,0:T(8,128)(2,1)} %collective-permute-done.3.refs_10_), channel_id=1, source_target_pairs={{0,2},{2,0},{1,3},{3,1},{4,6},{6,4},{5,7},{7,5},{8,10},{10,8},{9,1... | collective-permute-start | bytes 2285576 | tf_op jit(solution)/shard_map/ppermute | solution.py:281
  59.9 0.0 collective-permute-start.4
  59.9 2.3 %collective-permute-start.5 = (bf16[8,64,128]{2,1,0:T(8,128)(2,1)S(1)}, bf16[8,64,128]{2,1,0:T(8,128)(2,1)S(1)}, u32[]{:S(2)}, u32[]{:S(2)}) collective-permute-start(bf16[8,64,128]{2,1,0:T(8,128)(2,1)S(1)} %get-tuple-element.26), channel_id=1, source_target_pairs={{0,16},{16,0},{1,17},{17,1},{2,18},{18,2},{3,19},{19,3},{4,20},{20... | collective-permute-start | bytes 393224 | tf_op jit(solution)/shard_map/ppermute | solution.py:283
  62.3 1.8 %collective-permute-done.8.refs_9_ = bf16[124,3072]{1,0:T(8,128)(2,1)} collective-permute-done((bf16[124,3072]{1,0:T(8,128)(2,1)S(1)}, bf16[124,3072]{1,0:T(8,128)(2,1)}, u32[]{:S(2)}, u32[]{:S(2)}) %collective-permute-start.8) | collective-permute-done | bytes 761888 | tf_op jit(solution)/shard_map/ppermute | solution.py:275
  64.1 1.6 %collective-permute-start.6 = (bf16[8,64,128]{2,1,0:T(8,128)(2,1)S(1)}, bf16[8,64,128]{2,1,0:T(8,128)(2,1)S(1)}, u32[]{:S(2)}, u32[]{:S(2)}) collective-permute-start(bf16[8,64,128]{2,1,0:T(8,128)(2,1)S(1)} %get-tuple-element.27), channel_id=1, source_target_pairs={{0,17},{1,16},{16,1},{17,0},{2,19},{3,18},{18,3},{19,2},{4,21},{5,... | collective-permute-start | bytes 393224 | tf_op jit(solution)/shard_map/ppermute | solution.py:284
  65.7 0.0 collective-permute-done.7.refs_7_
  65.7 0.0 collective-permute-done.4.refs_1_
  65.7 0.0 copy-start.5
  65.7 7.0 %collective-permute-done.5.refs_2_ = bf16[8,64,128]{2,1,0:T(8,128)(2,1)S(1)} collective-permute-done((bf16[8,64,128]{2,1,0:T(8,128)(2,1)S(1)}, bf16[8,64,128]{2,1,0:T(8,128)(2,1)S(1)}, u32[]{:S(2)}, u32[]{:S(2)}) %collective-permute-start.5) | collective-permute-done | bytes 131104 | tf_op jit(solution)/shard_map/ppermute | solution.py:283
  72.7 0.0 copy-start.6
  72.7 2.0 %collective-permute-done.6.refs_3_ = bf16[8,64,128]{2,1,0:T(8,128)(2,1)S(1)} collective-permute-done((bf16[8,64,128]{2,1,0:T(8,128)(2,1)S(1)}, bf16[8,64,128]{2,1,0:T(8,128)(2,1)S(1)}, u32[]{:S(2)}, u32[]{:S(2)}) %collective-permute-start.6) | collective-permute-done | bytes 131104 | tf_op jit(solution)/shard_map/ppermute | solution.py:284
  74.8 0.0 copy-start.7
  74.8 3.0 %collective-permute-done.9.refs_11_ = bf16[124,3072]{1,0:T(8,128)(2,1)S(1)} collective-permute-done((bf16[124,3072]{1,0:T(8,128)(2,1)}, bf16[124,3072]{1,0:T(8,128)(2,1)S(1)}, u32[]{:S(2)}, u32[]{:S(2)}) %collective-permute-start.9) | collective-permute-done | bytes 761888 | tf_op jit(solution)/shard_map/ppermute | solution.py:281
  77.7 0.0 copy-done.1
  77.7 0.0 copy-done.2
  77.7 0.0 copy-done.3
  77.7 0.0 copy-done.5
  77.8 0.0 copy-done.6
  77.8 0.0 copy-done.7
  77.8 0.0 copy-start.4
  77.8 0.9 copy-done.4
  78.7 7.8 %second_quarter.1 = (f32[64,3072]{1,0:T(8,128)}, bf16[64,3072]{1,0:T(8,128)(2,1)}, f32[64,3072]{1,0:T(8,128)}, bf16[64,3072]{1,0:T(8,128)(2,1)}) custom-call(bf16[8,64,128]{2,1,0:T(8,128)(2,1)} %copy-done, bf16[8,64,128]{2,1,0:T(8,128)(2,1)} %copy-done.5, bf16[8,64,128]{2,1,0:T(8,128)(2,1)} %copy-done.6, bf16[8,64,128]{2,1,0:T(8,128)(2,1)} %copy-done.7, ...), custom_call_target="tpu_custom_call" | custom-call | flops 1560281088 | bytes 8000000 | tf_op jit(solution)/shard_map/second_quarter/pallas_call | solution.py:233
  86.5 0.1 collective-permute-start.10
  86.6 1.9 %collective-permute-done.10 = bf16[64,3072]{1,0:T(8,128)(2,1)S(1)} collective-permute-done((bf16[64,3072]{1,0:T(8,128)(2,1)}, bf16[64,3072]{1,0:T(8,128)(2,1)S(1)}, u32[]{:S(2)}, u32[]{:S(2)}) %collective-permute-start.10) | collective-permute-done | bytes 393248 | tf_op jit(solution)/shard_map/ppermute | solution.py:290
  88.5 1.2 %add_convert_fusion.1 = bf16[64,3072]{1,0:T(8,128)(2,1)S(1)} fusion(f32[64,3072]{1,0:T(8,128)} %get-tuple-element.33, bf16[64,3072]{1,0:T(8,128)(2,1)S(1)} %collective-permute-done.10), kind=kLoop, calls=%fused_computation.1 | loop fusion | flops 589824 | bytes 1572864 | tf_op jit(solution)/shard_map/convert_element_type | solution.py:291
  89.7 0.2 collective-permute-start.11
  89.9 2.6 %collective-permute-start.12 = (bf16[64,3072]{1,0:T(8,128)(2,1)S(1)}, bf16[64,3072]{1,0:T(8,128)(2,1)S(1)}, u32[]{:S(2)}, u32[]{:S(2)}) collective-permute-start(bf16[64,3072]{1,0:T(8,128)(2,1)S(1)} %add_convert_fusion.1), channel_id=1, source_target_pairs={{0,16},{16,0},{1,17},{17,1},{2,18},{18,2},{3,19},{19,3},{4,20},{20... | collective-permute-start | bytes 1179656 | tf_op jit(solution)/shard_map/ppermute | solution.py:293
  92.6 0.0 collective-permute-done.11
  92.6 18.1 %collective-permute-done.12 = bf16[64,3072]{1,0:T(8,128)(2,1)S(1)} collective-permute-done((bf16[64,3072]{1,0:T(8,128)(2,1)S(1)}, bf16[64,3072]{1,0:T(8,128)(2,1)S(1)}, u32[]{:S(2)}, u32[]{:S(2)}) %collective-permute-start.12) | collective-permute-done | bytes 393248 | tf_op jit(solution)/shard_map/ppermute | solution.py:293
  110.7 2.0 %add_convert_fusion = bf16[64,3072]{1,0:T(8,128)(2,1)} fusion(bf16[64,3072]{1,0:T(8,128)(2,1)S(1)} %collective-permute-done.12, f32[64,3072]{1,0:T(8,128)} %get-tuple-element.31, bf16[64,3072]{1,0:T(8,128)(2,1)S(1)} %collective-permute-done.11), kind=kLoop, calls=%fused_computation | loop fusion | flops 983040 | bytes 1966080 | tf_op jit(solution)/shard_map/convert_element_type | solution.py:296
  (6 shorter events, 0.1 us)
Async XLA Ops:
  0.0 27.4 %copy-start.9 = (s32[256]{0:T(256)S(1)}, s32[256]{0:T(256)}, u32[]{:S(2)}) copy-start(s32[256]{0:T(256)} %refs_1_.1) | copy-start | bytes 3076
  0.0 29.3 %copy-start.8 = (s32[2,256]{1,0:T(2,128)S(1)}, s32[2,256]{1,0:T(2,128)}, u32[]{:S(2)}) copy-start(s32[2,256]{1,0:T(2,128)} %refs_2_.1) | copy-start | bytes 6148
  0.0 20.7 %collective-permute-start.1 = (bf16[124,3072]{1,0:T(8,128)(2,1)}, bf16[124,3072]{1,0:T(8,128)(2,1)S(1)}, u32[]{:S(2)}, u32[]{:S(2)}) collective-permute-start(bf16[124,3072]{1,0:T(8,128)(2,1)} %refs_4_.3), channel_id=1, source_target_pairs={{0,4},{4,0},{1,5},{5,1},{2,6},{6,2},{3,7},{7,3},{8,12},{12,8},{9,1... | collective-permute-start | bytes 2285576 | tf_op jit(solution)/shard_map/ppermute | solution.py:262
  3.0 19.2 %collective-permute-start = (bf16[124,3072]{1,0:T(8,128)(2,1)}, bf16[124,3072]{1,0:T(8,128)(2,1)S(1)}, u32[]{:S(2)}, u32[]{:S(2)}) collective-permute-start(bf16[124,3072]{1,0:T(8,128)(2,1)} %refs_4_.3), channel_id=1, source_target_pairs={{0,8},{8,0},{1,9},{9,1},{2,10},{10,2},{3,11},{11,3},{4,12},{12,4},... | collective-permute-start | bytes 2285576 | tf_op jit(solution)/shard_map/ppermute | solution.py:261
  4.5 18.9 %collective-permute-start.2 = (bf16[124,3072]{1,0:T(8,128)(2,1)}, bf16[124,3072]{1,0:T(8,128)(2,1)S(1)}, u32[]{:S(2)}, u32[]{:S(2)}) collective-permute-start(bf16[124,3072]{1,0:T(8,128)(2,1)} %refs_4_.3), channel_id=1, source_target_pairs={{0,2},{2,0},{1,3},{3,1},{4,6},{6,4},{5,7},{7,5},{8,10},{10,8},{9,1... | collective-permute-start | bytes 2285576 | tf_op jit(solution)/shard_map/ppermute | solution.py:263
  20.7 57.0 %copy-start.1 = (bf16[124,3072]{1,0:T(8,128)(2,1)}, bf16[124,3072]{1,0:T(8,128)(2,1)S(1)}, u32[]{:S(2)}) copy-start(bf16[124,3072]{1,0:T(8,128)(2,1)S(1)} %collective-permute-done.1.refs_6_) | copy-start | bytes 2285572
  22.2 55.6 %copy-start.2 = (bf16[124,3072]{1,0:T(8,128)(2,1)}, bf16[124,3072]{1,0:T(8,128)(2,1)S(1)}, u32[]{:S(2)}) copy-start(bf16[124,3072]{1,0:T(8,128)(2,1)S(1)} %collective-permute-done.refs_8_) | copy-start | bytes 2285572
  23.5 54.3 %copy-start.3 = (bf16[124,3072]{1,0:T(8,128)(2,1)}, bf16[124,3072]{1,0:T(8,128)(2,1)S(1)}, u32[]{:S(2)}) copy-start(bf16[124,3072]{1,0:T(8,128)(2,1)S(1)} %collective-permute-done.2.refs_5_) | copy-start | bytes 2285572
  23.5 30.2 %all-to-all-start = ((bf16[32,2,64,128]{3,2,1,0:T(8,128)(2,1)}), bf16[32,2,64,128]{3,2,1,0:T(8,128)(2,1)S(1)}, u32[]{:S(2)}, u32[]{:S(2)}) async-start(bf16[32,2,64,128]{3,2,1,0:T(8,128)(2,1)} %first_quarter.1), calls=%async_computation | async-start | bytes 2097152 | tf_op jit(solution)/shard_map/all_to_all | solution.py:273
  27.5 31.0 %collective-permute-start.3 = (bf16[124,3072]{1,0:T(8,128)(2,1)S(1)}, bf16[124,3072]{1,0:T(8,128)(2,1)}, u32[]{:S(2)}, u32[]{:S(2)}) collective-permute-start(bf16[124,3072]{1,0:T(8,128)(2,1)S(1)} %collective-permute-done.refs_8_), channel_id=1, source_target_pairs={{0,4},{4,0},{1,5},{5,1},{2,6},{6,2},{3,7},{7,3},{8,12},{12,8},{9,1... | collective-permute-start | bytes 2285576 | tf_op jit(solution)/shard_map/ppermute | solution.py:274
  29.9 34.2 %collective-permute-start.8 = (bf16[124,3072]{1,0:T(8,128)(2,1)S(1)}, bf16[124,3072]{1,0:T(8,128)(2,1)}, u32[]{:S(2)}, u32[]{:S(2)}) collective-permute-start(bf16[124,3072]{1,0:T(8,128)(2,1)S(1)} %collective-permute-done.2.refs_5_), channel_id=1, source_target_pairs={{0,8},{8,0},{1,9},{9,1},{2,10},{10,2},{3,11},{11,3},{4,12},{12,4},... | collective-permute-start | bytes 2285576 | tf_op jit(solution)/shard_map/ppermute | solution.py:275
  31.7 34.0 %collective-permute-start.7 = (bf16[124,3072]{1,0:T(8,128)(2,1)S(1)}, bf16[124,3072]{1,0:T(8,128)(2,1)}, u32[]{:S(2)}, u32[]{:S(2)}) collective-permute-start(bf16[124,3072]{1,0:T(8,128)(2,1)S(1)} %collective-permute-done.1.refs_6_), channel_id=1, source_target_pairs={{0,2},{2,0},{1,3},{3,1},{4,6},{6,4},{5,7},{7,5},{8,10},{10,8},{9,1... | collective-permute-start | bytes 2285576 | tf_op jit(solution)/shard_map/ppermute | solution.py:276
  57.8 0.6 copy-start
  58.4 19.3 %collective-permute-start.9 = (bf16[124,3072]{1,0:T(8,128)(2,1)}, bf16[124,3072]{1,0:T(8,128)(2,1)S(1)}, u32[]{:S(2)}, u32[]{:S(2)}) collective-permute-start(bf16[124,3072]{1,0:T(8,128)(2,1)} %collective-permute-done.3.refs_10_), channel_id=1, source_target_pairs={{0,2},{2,0},{1,3},{3,1},{4,6},{6,4},{5,7},{7,5},{8,10},{10,8},{9,1... | collective-permute-start | bytes 2285576 | tf_op jit(solution)/shard_map/ppermute | solution.py:281
  59.9 5.8 %collective-permute-start.4 = (bf16[8,64,128]{2,1,0:T(8,128)(2,1)S(1)}, bf16[8,64,128]{2,1,0:T(8,128)(2,1)S(1)}, u32[]{:S(2)}, u32[]{:S(2)}) collective-permute-start(bf16[8,64,128]{2,1,0:T(8,128)(2,1)S(1)} %get-tuple-element.25), channel_id=1, source_target_pairs={{0,1},{1,0},{2,3},{3,2},{4,5},{5,4},{6,7},{7,6},{8,9},{9,8},{10,11... | collective-permute-start | bytes 393224 | tf_op jit(solution)/shard_map/ppermute | solution.py:285
  59.9 12.8 %collective-permute-start.5 = (bf16[8,64,128]{2,1,0:T(8,128)(2,1)S(1)}, bf16[8,64,128]{2,1,0:T(8,128)(2,1)S(1)}, u32[]{:S(2)}, u32[]{:S(2)}) collective-permute-start(bf16[8,64,128]{2,1,0:T(8,128)(2,1)S(1)} %get-tuple-element.26), channel_id=1, source_target_pairs={{0,16},{16,0},{1,17},{17,1},{2,18},{18,2},{3,19},{19,3},{4,20},{20... | collective-permute-start | bytes 393224 | tf_op jit(solution)/shard_map/ppermute | solution.py:283
  64.1 10.7 %collective-permute-start.6 = (bf16[8,64,128]{2,1,0:T(8,128)(2,1)S(1)}, bf16[8,64,128]{2,1,0:T(8,128)(2,1)S(1)}, u32[]{:S(2)}, u32[]{:S(2)}) collective-permute-start(bf16[8,64,128]{2,1,0:T(8,128)(2,1)S(1)} %get-tuple-element.27), channel_id=1, source_target_pairs={{0,17},{1,16},{16,1},{17,0},{2,19},{3,18},{18,3},{19,2},{4,21},{5,... | collective-permute-start | bytes 393224 | tf_op jit(solution)/shard_map/ppermute | solution.py:284
  65.7 12.0 %copy-start.5 = (bf16[8,64,128]{2,1,0:T(8,128)(2,1)}, bf16[8,64,128]{2,1,0:T(8,128)(2,1)S(1)}, u32[]{:S(2)}) copy-start(bf16[8,64,128]{2,1,0:T(8,128)(2,1)S(1)} %collective-permute-done.4.refs_1_) | copy-start | bytes 393220
  72.7 5.0 %copy-start.6 = (bf16[8,64,128]{2,1,0:T(8,128)(2,1)}, bf16[8,64,128]{2,1,0:T(8,128)(2,1)S(1)}, u32[]{:S(2)}) copy-start(bf16[8,64,128]{2,1,0:T(8,128)(2,1)S(1)} %collective-permute-done.5.refs_2_) | copy-start | bytes 393220
  74.8 3.0 %copy-start.7 = (bf16[8,64,128]{2,1,0:T(8,128)(2,1)}, bf16[8,64,128]{2,1,0:T(8,128)(2,1)S(1)}, u32[]{:S(2)}) copy-start(bf16[8,64,128]{2,1,0:T(8,128)(2,1)S(1)} %collective-permute-done.6.refs_3_) | copy-start | bytes 393220
  77.8 0.9 copy-start.4
  86.5 2.0 %collective-permute-start.10 = (bf16[64,3072]{1,0:T(8,128)(2,1)}, bf16[64,3072]{1,0:T(8,128)(2,1)S(1)}, u32[]{:S(2)}, u32[]{:S(2)}) collective-permute-start(bf16[64,3072]{1,0:T(8,128)(2,1)} %get-tuple-element.34), channel_id=1, source_target_pairs={{0,1},{1,0},{2,3},{3,2},{4,5},{5,4},{6,7},{7,6},{8,9},{9,8},{10,11... | collective-permute-start | bytes 1179656 | tf_op jit(solution)/shard_map/ppermute | solution.py:290
  89.7 2.8 %collective-permute-start.11 = (bf16[64,3072]{1,0:T(8,128)(2,1)}, bf16[64,3072]{1,0:T(8,128)(2,1)S(1)}, u32[]{:S(2)}, u32[]{:S(2)}) collective-permute-start(bf16[64,3072]{1,0:T(8,128)(2,1)} %get-tuple-element.35), channel_id=1, source_target_pairs={{0,1},{1,0},{2,3},{3,2},{4,5},{5,4},{6,7},{7,6},{8,9},{9,8},{10,11... | collective-permute-start | bytes 1179656 | tf_op jit(solution)/shard_map/ppermute | solution.py:294
  89.9 20.7 %collective-permute-start.12 = (bf16[64,3072]{1,0:T(8,128)(2,1)S(1)}, bf16[64,3072]{1,0:T(8,128)(2,1)S(1)}, u32[]{:S(2)}, u32[]{:S(2)}) collective-permute-start(bf16[64,3072]{1,0:T(8,128)(2,1)S(1)} %add_convert_fusion.1), channel_id=1, source_target_pairs={{0,16},{16,0},{1,17},{17,1},{2,18},{18,2},{3,19},{19,3},{4,20},{20... | collective-permute-start | bytes 1179656 | tf_op jit(solution)/shard_map/ppermute | solution.py:293

commit v3 on v2

--- a/solution.py
+++ b/solution.py
@@ -269,14 +269,13 @@
     nu = jnp.where(jnp.any(chosen, axis=2), jnp.sum(jnp.where(chosen, nu_table, 0), axis=2), shell_count)
     me = jnp.reshape(device_index, (1,)).astype(jnp.int32)
     quarter = first_quarter(me, live_flags, shell_pairs, occ_coef.T, tiles, device_count)
-    quarter, by_near, by_row, by_col = lax.optimization_barrier((quarter, by_near, by_row, by_col))
     got = lax.all_to_all(quarter, AXES, split_axis=0, concat_axis=0, tiled=True)
     near_row = lax.ppermute(by_near, ROW, swap)
     near_col = lax.ppermute(by_col, NEAR, swap)
     row_col = lax.ppermute(by_row, COL, swap)
 
     at = jnp.stack([lax.axis_index(axis) for axis in AXES])
-    own, to_core, to_far, to_both = sum_shells(nu.reshape(-1), at, got, shell_size, shell_count, depth)
+    own, to_core, to_far, to_both = sum_shells(shell_list(nu).reshape(-1), at, got, shell_size, shell_count, depth)
     own, near_row = lax.optimization_barrier((own, near_row))
     all_three = lax.ppermute(near_row, COL, swap)
     panels = [vir_coef, by_col, by_row, row_col, by_near, near_col, near_row, all_three]

time: 113 us -> 105 us (0.929)
  waiting for transfers between devices: 61.7 us -> 54.5 us
  starting transfers between devices: 23.1 us -> 20 us
  Pallas kernels: 22 us -> 23.3 us
    all_to_all x1, waiting for transfers between devices: 20.6 us -> 15.6 us  [on_device(): got = lax.all_to_all(quarter, AXES, split_axis=0, concat_axis=0, tiled=True)]
    ppermute x1, waiting for transfers between devices: 0.02 us -> 1.51 us  [on_device(): near_row = lax.ppermute(by_near, ROW, swap)]
    ppermute x1, starting transfers between devices: 2.97 us -> 1.52 us  [on_device(): by_row = lax.ppermute(vir_coef, ROW, swap)]
    ppermute x1, starting transfers between devices: 1.49 us -> 2.94 us  [on_device(): by_col = lax.ppermute(vir_coef, COL, swap)]
    ppermute x1, starting transfers between devices: 1.46 us -> 0.02 us  [on_device(): row_col = lax.ppermute(by_row, COL, swap)]
    pallas_call x0 -> x1, Pallas kernels: none -> 1.32 us  [shell_list(): pl.pallas_call(shell_list_body, out_shape=jax.ShapeDtypeStruct(nu.shape,...]
    ppermute x1, waiting for transfers between devices: 1.46 us -> 0.17 us  [on_device(): by_near = lax.ppermute(vir_coef, NEAR, swap)]
    ppermute x1, waiting for transfers between devices: 1.29 us -> 0.1 us  [on_device(): by_col = lax.ppermute(vir_coef, COL, swap)]
  transfers between devices with their start and end apart: 14 -> 14, of which waited for: 10 -> 11; matrix products, arithmetic and copies ran while one was open for 1% -> 2% of each run, Pallas kernels for 13% -> 15%
where the time goes in v3:
time: 105 us
  waiting for transfers between devices  54.5 us (52%)
  Pallas kernels  23.3 us (22%)
  starting transfers between devices  20 us (19%)
  other arithmetic  4.05 us (4%)
  local copies, waits for them, and re-layouts  3.08 us (3%)
    ppermute x1, waiting for transfers between devices, on_device(): taken = lax.ppermute(far_part, FAR, swap)  18.3 us
    all_to_all x1, waiting for transfers between devices, on_device(): got = lax.all_to_all(quarter, AXES, split_axis=0, concat_axis=0, tiled=True)  15.6 us
    pallas_call x1, Pallas kernels, first_quarter(): pl.pallas_call(body, out_shape=jax.ShapeDtypeStruct(shape, jnp.bfloat16),...  10.1 us
    pallas_call x1, Pallas kernels, transform(): pl.pallas_call(body, out_shape=[jax.ShapeDtypeStruct((rows, columns), dty...  7.86 us
    ppermute x1, waiting for transfers between devices, on_device(): from_far = lax.ppermute(to_far, FAR, swap)  7.01 us
    pallas_call x1, Pallas kernels, sum_shells(): pl.pallas_call(body, out_shape=[jax.ShapeDtypeStruct((sources // 4, rows,...  4.03 us
    ppermute x1, waiting for transfers between devices, on_device(): by_row = lax.ppermute(vir_coef, ROW, swap)  3.55 us
    ppermute x1, waiting for transfers between devices, on_device(): all_three = lax.ppermute(near_row, COL, swap)  3.1 us
  transfers between devices with their start and end apart: 14, of which 11 were waited for; matrix products, arithmetic and copies ran while one was open for 2% of the time, Pallas kernels for 15%

profile of v3, /device:TPU:0, one launch (start us, length us, event | category | flops | bytes accessed | tf_op | source)
XLA Modules:
  0.0 105.1 jit_solution(5223662658181974874)
XLA Ops:
  0.0 0.0 copy-start.9
  0.0 0.0 copy-start.8
  0.0 2.9 %collective-permute-start.5 = (bf16[124,3072]{1,0:T(8,128)(2,1)}, bf16[124,3072]{1,0:T(8,128)(2,1)S(1)}, u32[]{:S(2)}, u32[]{:S(2)}) collective-permute-start(bf16[124,3072]{1,0:T(8,128)(2,1)} %refs_4_.3), channel_id=1, source_target_pairs={{0,2},{2,0},{1,3},{3,1},{4,6},{6,4},{5,7},{7,5},{8,10},{10,8},{9,1... | collective-permute-start | bytes 2285576 | tf_op jit(solution)/shard_map/ppermute | solution.py:263
  2.9 1.6 %collective-permute-start = (bf16[124,3072]{1,0:T(8,128)(2,1)}, bf16[124,3072]{1,0:T(8,128)(2,1)S(1)}, u32[]{:S(2)}, u32[]{:S(2)}) collective-permute-start(bf16[124,3072]{1,0:T(8,128)(2,1)} %refs_4_.3), channel_id=1, source_target_pairs={{0,8},{8,0},{1,9},{9,1},{2,10},{10,2},{3,11},{11,3},{4,12},{12,4},... | collective-permute-start | bytes 2285576 | tf_op jit(solution)/shard_map/ppermute | solution.py:261
  4.5 1.5 %collective-permute-start.6 = (bf16[124,3072]{1,0:T(8,128)(2,1)}, bf16[124,3072]{1,0:T(8,128)(2,1)S(1)}, u32[]{:S(2)}, u32[]{:S(2)}) collective-permute-start(bf16[124,3072]{1,0:T(8,128)(2,1)} %refs_4_.3), channel_id=1, source_target_pairs={{0,4},{4,0},{1,5},{5,1},{2,6},{6,2},{3,7},{7,3},{8,12},{12,8},{9,1... | collective-permute-start | bytes 2285576 | tf_op jit(solution)/shard_map/ppermute | solution.py:262
  6.0 10.1 %first_quarter.1 = bf16[32,2,64,128]{3,2,1,0:T(8,128)(2,1)} custom-call(s32[1]{0:T(128)} %bitcast.5.refs_0_, s32[256]{0:T(256)} %refs_1_.1, s32[2,256]{1,0:T(2,128)} %refs_2_.1, bf16[32,3968]{1,0:T(8,128)(2,1)} %bitcast.8, bf16[8,64,64,64]{3,2,1,0:T(8,128)(2,1)} %refs_4_.2), custom_call_target="tpu_custom_call" | custom-call | flops 1000000000 | bytes 6000000 | tf_op jit(solution)/shard_map/first_quarter/pallas_call | solution.py:121
  16.1 3.0 %all-to-all-start = ((bf16[32,2,64,128]{3,2,1,0:T(8,128)(2,1)}), bf16[32,2,64,128]{3,2,1,0:T(8,128)(2,1)S(1)}, u32[]{:S(2)}, u32[]{:S(2)}) async-start(bf16[32,2,64,128]{3,2,1,0:T(8,128)(2,1)} %first_quarter.1), calls=%async_computation | async-start | bytes 2097152 | tf_op jit(solution)/shard_map/all_to_all | solution.py:272
  19.1 0.0 copy-done.9
  19.1 0.1 reduce_window_sum.13
  19.2 0.0 copy-done.8
  19.2 0.1 broadcast_in_dim.20
  19.3 0.1 copy.8
  19.4 0.1 copy.7
  19.5 0.2 reduce_window_sum.14
  19.6 0.1 copy.6
  19.8 0.1 copy.9
  19.9 0.1 copy.10
  20.0 0.6 broadcast_select_fusion.nu_ref
  20.6 0.1 collective-permute-done.5.refs_5_
  20.7 0.0 copy-start.1
  20.7 1.8 %collective-permute-start.8 = (bf16[124,3072]{1,0:T(8,128)(2,1)S(1)}, bf16[124,3072]{1,0:T(8,128)(2,1)}, u32[]{:S(2)}, u32[]{:S(2)}) collective-permute-start(bf16[124,3072]{1,0:T(8,128)(2,1)S(1)} %collective-permute-done.5.refs_5_), channel_id=1, source_target_pairs={{0,8},{8,0},{1,9},{9,1},{2,10},{10,2},{3,11},{11,3},{4,12},{12,4},... | collective-permute-start | bytes 2285576 | tf_op jit(solution)/shard_map/ppermute | solution.py:274
  22.5 0.2 collective-permute-done.refs_8_
  22.7 0.0 copy-start.2
  22.7 1.4 %collective-permute-start.1 = (bf16[124,3072]{1,0:T(8,128)(2,1)S(1)}, bf16[124,3072]{1,0:T(8,128)(2,1)}, u32[]{:S(2)}, u32[]{:S(2)}) collective-permute-start(bf16[124,3072]{1,0:T(8,128)(2,1)S(1)} %collective-permute-done.refs_8_), channel_id=1, source_target_pairs={{0,4},{4,0},{1,5},{5,1},{2,6},{6,2},{3,7},{7,3},{8,12},{12,8},{9,1... | collective-permute-start | bytes 2285576 | tf_op jit(solution)/shard_map/ppermute | solution.py:273
  24.1 1.3 %shell_list.1 = s32[32,4]{1,0:T(8,128)} custom-call(s32[32,4]{1,0:T(8,128)} %broadcast_select_fusion.nu_ref), custom_call_target="tpu_custom_call" | custom-call | flops 99999997952 | bytes 1000000 | tf_op jit(solution)/shard_map/shell_list/pallas_call | solution.py:57
  25.4 0.0 copy-done.1
  25.4 0.0 copy-done.2
  25.4 0.8 reshape.25.refs_0_
  26.2 0.1 stack.23.refs_1_
  26.3 3.6 %collective-permute-done.6.refs_6_ = bf16[124,3072]{1,0:T(8,128)(2,1)S(1)} collective-permute-done((bf16[124,3072]{1,0:T(8,128)(2,1)}, bf16[124,3072]{1,0:T(8,128)(2,1)S(1)}, u32[]{:S(2)}, u32[]{:S(2)}) %collective-permute-start.6) | collective-permute-done | bytes 761888 | tf_op jit(solution)/shard_map/ppermute | solution.py:262
  29.9 0.0 copy-start.3
  29.9 0.0 collective-permute-start.7
  29.9 15.6 %all-to-all-done.refs_2_ = bf16[32,2,64,128]{3,2,1,0:T(8,128)(2,1)S(1)} async-done(((bf16[32,2,64,128]{3,2,1,0:T(8,128)(2,1)}), bf16[32,2,64,128]{3,2,1,0:T(8,128)(2,1)S(1)}, u32[]{:S(2)}, u32[]{:S(2)}) %all-to-all-start) | async-done | bytes 1048608 | tf_op jit(solution)/shard_map/all_to_all | solution.py:272
  45.4 4.0 %sum_shells.1 = (bf16[8,64,128]{2,1,0:T(8,128)(2,1)S(1)}, bf16[8,64,128]{2,1,0:T(8,128)(2,1)S(1)}, bf16[8,64,128]{2,1,0:T(8,128)(2,1)S(1)}, bf16[8,64,128]{2,1,0:T(8,128)(2,1)S(1)}) custom-call(s32[128]{0:T(128)S(1)} %reshape.25.refs_0_, s32[5]{0:T(128)S(1)} %stack.23.refs_1_, bf16[32,2,64,128]{3,2,1,0:T(8,128)(2,1)S(1)} %all-to-all-done.refs_2_), custom_call_target="tpu_custom_call" | custom-call | flops 10000000 | bytes 4000000 | tf_op jit(solution)/shard_map/sum_shells/pallas_call | solution.py:182
  49.5 0.0 copy-start
  49.5 0.6 copy-done
  50.1 1.5 %collective-permute-done.1.refs_10_ = bf16[124,3072]{1,0:T(8,128)(2,1)} collective-permute-done((bf16[124,3072]{1,0:T(8,128)(2,1)S(1)}, bf16[124,3072]{1,0:T(8,128)(2,1)}, u32[]{:S(2)}, u32[]{:S(2)}) %collective-permute-start.1) | collective-permute-done | bytes 761888 | tf_op jit(solution)/shard_map/ppermute | solution.py:273
  51.6 0.5 collective-permute-start.9
  52.2 0.0 collective-permute-start.2
  52.2 2.6 %collective-permute-start.3 = (bf16[8,64,128]{2,1,0:T(8,128)(2,1)S(1)}, bf16[8,64,128]{2,1,0:T(8,128)(2,1)S(1)}, u32[]{:S(2)}, u32[]{:S(2)}) collective-permute-start(bf16[8,64,128]{2,1,0:T(8,128)(2,1)S(1)} %get-tuple-element.20), channel_id=1, source_target_pairs={{0,16},{16,0},{1,17},{17,1},{2,18},{18,2},{3,19},{19,3},{4,20},{20... | collective-permute-start | bytes 393224 | tf_op jit(solution)/shard_map/ppermute | solution.py:282
  54.8 1.2 %collective-permute-done.8.refs_9_ = bf16[124,3072]{1,0:T(8,128)(2,1)} collective-permute-done((bf16[124,3072]{1,0:T(8,128)(2,1)S(1)}, bf16[124,3072]{1,0:T(8,128)(2,1)}, u32[]{:S(2)}, u32[]{:S(2)}) %collective-permute-start.8) | collective-permute-done | bytes 761888 | tf_op jit(solution)/shard_map/ppermute | solution.py:274
  56.0 2.0 %collective-permute-start.4 = (bf16[8,64,128]{2,1,0:T(8,128)(2,1)S(1)}, bf16[8,64,128]{2,1,0:T(8,128)(2,1)S(1)}, u32[]{:S(2)}, u32[]{:S(2)}) collective-permute-start(bf16[8,64,128]{2,1,0:T(8,128)(2,1)S(1)} %get-tuple-element.21), channel_id=1, source_target_pairs={{0,17},{1,16},{16,1},{17,0},{2,19},{3,18},{18,3},{19,2},{4,21},{5,... | collective-permute-start | bytes 393224 | tf_op jit(solution)/shard_map/ppermute | solution.py:283
  58.0 0.0 collective-permute-done.7.refs_7_
  58.0 0.0 collective-permute-done.2.refs_1_
  58.0 0.0 copy-start.5
  58.0 7.0 %collective-permute-done.3.refs_2_ = bf16[8,64,128]{2,1,0:T(8,128)(2,1)S(1)} collective-permute-done((bf16[8,64,128]{2,1,0:T(8,128)(2,1)S(1)}, bf16[8,64,128]{2,1,0:T(8,128)(2,1)S(1)}, u32[]{:S(2)}, u32[]{:S(2)}) %collective-permute-start.3) | collective-permute-done | bytes 131104 | tf_op jit(solution)/shard_map/ppermute | solution.py:282
  65.0 0.0 copy-start.6
  65.0 2.0 %collective-permute-done.4.refs_3_ = bf16[8,64,128]{2,1,0:T(8,128)(2,1)S(1)} collective-permute-done((bf16[8,64,128]{2,1,0:T(8,128)(2,1)S(1)}, bf16[8,64,128]{2,1,0:T(8,128)(2,1)S(1)}, u32[]{:S(2)}, u32[]{:S(2)}) %collective-permute-start.4) | collective-permute-done | bytes 131104 | tf_op jit(solution)/shard_map/ppermute | solution.py:283
  67.0 3.1 %collective-permute-done.9.refs_11_ = bf16[124,3072]{1,0:T(8,128)(2,1)S(1)} collective-permute-done((bf16[124,3072]{1,0:T(8,128)(2,1)}, bf16[124,3072]{1,0:T(8,128)(2,1)S(1)}, u32[]{:S(2)}, u32[]{:S(2)}) %collective-permute-start.9) | collective-permute-done | bytes 761888 | tf_op jit(solution)/shard_map/ppermute | solution.py:280
  70.1 0.0 copy-done.3
  70.1 0.0 copy-done.5
  70.1 0.0 copy-done.6
  70.1 0.0 copy-done.7
  70.2 0.0 copy-start.4
  70.2 0.9 copy-done.4
  71.1 7.9 %second_quarter.1 = (f32[64,3072]{1,0:T(8,128)}, bf16[64,3072]{1,0:T(8,128)(2,1)}, f32[64,3072]{1,0:T(8,128)}, bf16[64,3072]{1,0:T(8,128)(2,1)}) custom-call(bf16[8,64,128]{2,1,0:T(8,128)(2,1)} %copy-done, bf16[8,64,128]{2,1,0:T(8,128)(2,1)} %copy-done.5, bf16[8,64,128]{2,1,0:T(8,128)(2,1)} %copy-done.6, bf16[8,64,128]{2,1,0:T(8,128)(2,1)} %copy-done.7, ...), custom_call_target="tpu_custom_call" | custom-call | flops 1560281088 | bytes 8000000 | tf_op jit(solution)/shard_map/second_quarter/pallas_call | solution.py:233
  78.9 0.1 collective-permute-start.10
  79.0 1.9 %collective-permute-done.10 = bf16[64,3072]{1,0:T(8,128)(2,1)S(1)} collective-permute-done((bf16[64,3072]{1,0:T(8,128)(2,1)}, bf16[64,3072]{1,0:T(8,128)(2,1)S(1)}, u32[]{:S(2)}, u32[]{:S(2)}) %collective-permute-start.10) | collective-permute-done | bytes 393248 | tf_op jit(solution)/shard_map/ppermute | solution.py:289
  80.9 1.2 %add_convert_fusion.1 = bf16[64,3072]{1,0:T(8,128)(2,1)S(1)} fusion(f32[64,3072]{1,0:T(8,128)} %get-tuple-element.25, bf16[64,3072]{1,0:T(8,128)(2,1)S(1)} %collective-permute-done.10), kind=kLoop, calls=%fused_computation.1 | loop fusion | flops 589824 | bytes 1572864 | tf_op jit(solution)/shard_map/convert_element_type | solution.py:290
  82.1 0.2 collective-permute-start.11
  82.3 2.4 %collective-permute-start.12 = (bf16[64,3072]{1,0:T(8,128)(2,1)S(1)}, bf16[64,3072]{1,0:T(8,128)(2,1)S(1)}, u32[]{:S(2)}, u32[]{:S(2)}) collective-permute-start(bf16[64,3072]{1,0:T(8,128)(2,1)S(1)} %add_convert_fusion.1), channel_id=1, source_target_pairs={{0,16},{16,0},{1,17},{17,1},{2,18},{18,2},{3,19},{19,3},{4,20},{20... | collective-permute-start | bytes 1179656 | tf_op jit(solution)/shard_map/ppermute | solution.py:292
  84.7 0.0 collective-permute-done.11
  84.7 18.3 %collective-permute-done.12 = bf16[64,3072]{1,0:T(8,128)(2,1)S(1)} collective-permute-done((bf16[64,3072]{1,0:T(8,128)(2,1)S(1)}, bf16[64,3072]{1,0:T(8,128)(2,1)S(1)}, u32[]{:S(2)}, u32[]{:S(2)}) %collective-permute-start.12) | collective-permute-done | bytes 393248 | tf_op jit(solution)/shard_map/ppermute | solution.py:292
  103.1 2.0 %add_convert_fusion = bf16[64,3072]{1,0:T(8,128)(2,1)} fusion(bf16[64,3072]{1,0:T(8,128)(2,1)S(1)} %collective-permute-done.12, f32[64,3072]{1,0:T(8,128)} %get-tuple-element.23, bf16[64,3072]{1,0:T(8,128)(2,1)S(1)} %collective-permute-done.11), kind=kLoop, calls=%fused_computation | loop fusion | flops 983040 | bytes 1966080 | tf_op jit(solution)/shard_map/convert_element_type | solution.py:295
  (6 shorter events, 0.1 us)
Async XLA Ops:
  0.0 19.1 %copy-start.9 = (s32[256]{0:T(256)S(1)}, s32[256]{0:T(256)}, u32[]{:S(2)}) copy-start(s32[256]{0:T(256)} %refs_1_.1) | copy-start | bytes 3076
  0.0 19.2 %copy-start.8 = (s32[2,256]{1,0:T(2,128)S(1)}, s32[2,256]{1,0:T(2,128)}, u32[]{:S(2)}) copy-start(s32[2,256]{1,0:T(2,128)} %refs_2_.1) | copy-start | bytes 6148
  0.0 20.7 %collective-permute-start.5 = (bf16[124,3072]{1,0:T(8,128)(2,1)}, bf16[124,3072]{1,0:T(8,128)(2,1)S(1)}, u32[]{:S(2)}, u32[]{:S(2)}) collective-permute-start(bf16[124,3072]{1,0:T(8,128)(2,1)} %refs_4_.3), channel_id=1, source_target_pairs={{0,2},{2,0},{1,3},{3,1},{4,6},{6,4},{5,7},{7,5},{8,10},{10,8},{9,1... | collective-permute-start | bytes 2285576 | tf_op jit(solution)/shard_map/ppermute | solution.py:263
  2.9 19.8 %collective-permute-start = (bf16[124,3072]{1,0:T(8,128)(2,1)}, bf16[124,3072]{1,0:T(8,128)(2,1)S(1)}, u32[]{:S(2)}, u32[]{:S(2)}) collective-permute-start(bf16[124,3072]{1,0:T(8,128)(2,1)} %refs_4_.3), channel_id=1, source_target_pairs={{0,8},{8,0},{1,9},{9,1},{2,10},{10,2},{3,11},{11,3},{4,12},{12,4},... | collective-permute-start | bytes 2285576 | tf_op jit(solution)/shard_map/ppermute | solution.py:261
  4.5 25.3 %collective-permute-start.6 = (bf16[124,3072]{1,0:T(8,128)(2,1)}, bf16[124,3072]{1,0:T(8,128)(2,1)S(1)}, u32[]{:S(2)}, u32[]{:S(2)}) collective-permute-start(bf16[124,3072]{1,0:T(8,128)(2,1)} %refs_4_.3), channel_id=1, source_target_pairs={{0,4},{4,0},{1,5},{5,1},{2,6},{6,2},{3,7},{7,3},{8,12},{12,8},{9,1... | collective-permute-start | bytes 2285576 | tf_op jit(solution)/shard_map/ppermute | solution.py:262
  16.1 29.3 %all-to-all-start = ((bf16[32,2,64,128]{3,2,1,0:T(8,128)(2,1)}), bf16[32,2,64,128]{3,2,1,0:T(8,128)(2,1)S(1)}, u32[]{:S(2)}, u32[]{:S(2)}) async-start(bf16[32,2,64,128]{3,2,1,0:T(8,128)(2,1)} %first_quarter.1), calls=%async_computation | async-start | bytes 2097152 | tf_op jit(solution)/shard_map/all_to_all | solution.py:272
  20.7 4.7 %copy-start.1 = (bf16[124,3072]{1,0:T(8,128)(2,1)}, bf16[124,3072]{1,0:T(8,128)(2,1)S(1)}, u32[]{:S(2)}) copy-start(bf16[124,3072]{1,0:T(8,128)(2,1)S(1)} %collective-permute-done.5.refs_5_) | copy-start | bytes 2285572
  20.7 35.3 %collective-permute-start.8 = (bf16[124,3072]{1,0:T(8,128)(2,1)S(1)}, bf16[124,3072]{1,0:T(8,128)(2,1)}, u32[]{:S(2)}, u32[]{:S(2)}) collective-permute-start(bf16[124,3072]{1,0:T(8,128)(2,1)S(1)} %collective-permute-done.5.refs_5_), channel_id=1, source_target_pairs={{0,8},{8,0},{1,9},{9,1},{2,10},{10,2},{3,11},{11,3},{4,12},{12,4},... | collective-permute-start | bytes 2285576 | tf_op jit(solution)/shard_map/ppermute | solution.py:274
  22.7 2.7 %copy-start.2 = (bf16[124,3072]{1,0:T(8,128)(2,1)}, bf16[124,3072]{1,0:T(8,128)(2,1)S(1)}, u32[]{:S(2)}) copy-start(bf16[124,3072]{1,0:T(8,128)(2,1)S(1)} %collective-permute-done.refs_8_) | copy-start | bytes 2285572
  22.7 28.9 %collective-permute-start.1 = (bf16[124,3072]{1,0:T(8,128)(2,1)S(1)}, bf16[124,3072]{1,0:T(8,128)(2,1)}, u32[]{:S(2)}, u32[]{:S(2)}) collective-permute-start(bf16[124,3072]{1,0:T(8,128)(2,1)S(1)} %collective-permute-done.refs_8_), channel_id=1, source_target_pairs={{0,4},{4,0},{1,5},{5,1},{2,6},{6,2},{3,7},{7,3},{8,12},{12,8},{9,1... | collective-permute-start | bytes 2285576 | tf_op jit(solution)/shard_map/ppermute | solution.py:273
  29.9 40.3 %copy-start.3 = (bf16[124,3072]{1,0:T(8,128)(2,1)}, bf16[124,3072]{1,0:T(8,128)(2,1)S(1)}, u32[]{:S(2)}) copy-start(bf16[124,3072]{1,0:T(8,128)(2,1)S(1)} %collective-permute-done.6.refs_6_) | copy-start | bytes 2285572
  29.9 28.1 %collective-permute-start.7 = (bf16[124,3072]{1,0:T(8,128)(2,1)S(1)}, bf16[124,3072]{1,0:T(8,128)(2,1)}, u32[]{:S(2)}, u32[]{:S(2)}) collective-permute-start(bf16[124,3072]{1,0:T(8,128)(2,1)S(1)} %collective-permute-done.6.refs_6_), channel_id=1, source_target_pairs={{0,2},{2,0},{1,3},{3,1},{4,6},{6,4},{5,7},{7,5},{8,10},{10,8},{9,1... | collective-permute-start | bytes 2285576 | tf_op jit(solution)/shard_map/ppermute | solution.py:275
  49.5 0.6 copy-start
  51.6 18.5 %collective-permute-start.9 = (bf16[124,3072]{1,0:T(8,128)(2,1)}, bf16[124,3072]{1,0:T(8,128)(2,1)S(1)}, u32[]{:S(2)}, u32[]{:S(2)}) collective-permute-start(bf16[124,3072]{1,0:T(8,128)(2,1)} %collective-permute-done.1.refs_10_), channel_id=1, source_target_pairs={{0,2},{2,0},{1,3},{3,1},{4,6},{6,4},{5,7},{7,5},{8,10},{10,8},{9,1... | collective-permute-start | bytes 2285576 | tf_op jit(solution)/shard_map/ppermute | solution.py:280
  52.2 5.8 %collective-permute-start.2 = (bf16[8,64,128]{2,1,0:T(8,128)(2,1)S(1)}, bf16[8,64,128]{2,1,0:T(8,128)(2,1)S(1)}, u32[]{:S(2)}, u32[]{:S(2)}) collective-permute-start(bf16[8,64,128]{2,1,0:T(8,128)(2,1)S(1)} %get-tuple-element.19), channel_id=1, source_target_pairs={{0,1},{1,0},{2,3},{3,2},{4,5},{5,4},{6,7},{7,6},{8,9},{9,8},{10,11... | collective-permute-start | bytes 393224 | tf_op jit(solution)/shard_map/ppermute | solution.py:284
  52.2 12.8 %collective-permute-start.3 = (bf16[8,64,128]{2,1,0:T(8,128)(2,1)S(1)}, bf16[8,64,128]{2,1,0:T(8,128)(2,1)S(1)}, u32[]{:S(2)}, u32[]{:S(2)}) collective-permute-start(bf16[8,64,128]{2,1,0:T(8,128)(2,1)S(1)} %get-tuple-element.20), channel_id=1, source_target_pairs={{0,16},{16,0},{1,17},{17,1},{2,18},{18,2},{3,19},{19,3},{4,20},{20... | collective-permute-start | bytes 393224 | tf_op jit(solution)/shard_map/ppermute | solution.py:282
  56.0 11.1 %collective-permute-start.4 = (bf16[8,64,128]{2,1,0:T(8,128)(2,1)S(1)}, bf16[8,64,128]{2,1,0:T(8,128)(2,1)S(1)}, u32[]{:S(2)}, u32[]{:S(2)}) collective-permute-start(bf16[8,64,128]{2,1,0:T(8,128)(2,1)S(1)} %get-tuple-element.21), channel_id=1, source_target_pairs={{0,17},{1,16},{16,1},{17,0},{2,19},{3,18},{18,3},{19,2},{4,21},{5,... | collective-permute-start | bytes 393224 | tf_op jit(solution)/shard_map/ppermute | solution.py:283
  58.0 12.2 %copy-start.5 = (bf16[8,64,128]{2,1,0:T(8,128)(2,1)}, bf16[8,64,128]{2,1,0:T(8,128)(2,1)S(1)}, u32[]{:S(2)}) copy-start(bf16[8,64,128]{2,1,0:T(8,128)(2,1)S(1)} %collective-permute-done.2.refs_1_) | copy-start | bytes 393220
  65.0 5.1 %copy-start.6 = (bf16[8,64,128]{2,1,0:T(8,128)(2,1)}, bf16[8,64,128]{2,1,0:T(8,128)(2,1)S(1)}, u32[]{:S(2)}) copy-start(bf16[8,64,128]{2,1,0:T(8,128)(2,1)S(1)} %collective-permute-done.3.refs_2_) | copy-start | bytes 393220
  67.0 3.1 %copy-start.7 = (bf16[8,64,128]{2,1,0:T(8,128)(2,1)}, bf16[8,64,128]{2,1,0:T(8,128)(2,1)S(1)}, u32[]{:S(2)}) copy-start(bf16[8,64,128]{2,1,0:T(8,128)(2,1)S(1)} %collective-permute-done.4.refs_3_) | copy-start | bytes 393220
  70.2 0.9 copy-start.4
  78.9 2.0 %collective-permute-start.10 = (bf16[64,3072]{1,0:T(8,128)(2,1)}, bf16[64,3072]{1,0:T(8,128)(2,1)S(1)}, u32[]{:S(2)}, u32[]{:S(2)}) collective-permute-start(bf16[64,3072]{1,0:T(8,128)(2,1)} %get-tuple-element.26), channel_id=1, source_target_pairs={{0,1},{1,0},{2,3},{3,2},{4,5},{5,4},{6,7},{7,6},{8,9},{9,8},{10,11... | collective-permute-start | bytes 1179656 | tf_op jit(solution)/shard_map/ppermute | solution.py:289
  82.1 2.6 %collective-permute-start.11 = (bf16[64,3072]{1,0:T(8,128)(2,1)}, bf16[64,3072]{1,0:T(8,128)(2,1)S(1)}, u32[]{:S(2)}, u32[]{:S(2)}) collective-permute-start(bf16[64,3072]{1,0:T(8,128)(2,1)} %get-tuple-element.27), channel_id=1, source_target_pairs={{0,1},{1,0},{2,3},{3,2},{4,5},{5,4},{6,7},{7,6},{8,9},{9,8},{10,11... | collective-permute-start | bytes 1179656 | tf_op jit(solution)/shard_map/ppermute | solution.py:293
  82.3 20.7 %collective-permute-start.12 = (bf16[64,3072]{1,0:T(8,128)(2,1)S(1)}, bf16[64,3072]{1,0:T(8,128)(2,1)S(1)}, u32[]{:S(2)}, u32[]{:S(2)}) collective-permute-start(bf16[64,3072]{1,0:T(8,128)(2,1)S(1)} %add_convert_fusion.1), channel_id=1, source_target_pairs={{0,16},{16,0},{1,17},{17,1},{2,18},{18,2},{3,19},{19,3},{4,20},{20... | collective-permute-start | bytes 1179656 | tf_op jit(solution)/shard_map/ppermute | solution.py:292

commit v4 on v3

--- a/solution.py
+++ b/solution.py
@@ -98,10 +98,16 @@
         weight = jnp.where(diagonal[None], panel[:, None, :], 0.0).astype(jnp.bfloat16)
         weight = weight.reshape(occ_count * step, inner)
         copies[j].wait()
-        for part in range(shell_size // step):
-            block = held[j, :, part * step : (part + 1) * step, :].reshape(inner, ket_cols)
+        for part in range(0, shell_size // step, 2):
+            block = jnp.concatenate(
+                [held[j, :, p * step : (p + 1) * step, :].reshape(inner, ket_cols) for p in (part, part + 1)], axis=1
+            )
             result = jnp.dot(weight, block, preferred_element_type=jnp.float32)
-            turned[j % 2, :, part * step : (part + 1) * step, :] = result.reshape(occ_count, step, ket_cols)
+            for p in range(2):
+                at = (part + p) * step
+                turned[j % 2, :, at : at + step, :] = result[:, p * ket_cols : (p + 1) * ket_cols].reshape(
+                    occ_count, step, ket_cols
+                )
         if j % 2 == 1:
             for i in range(occ_count):
                 value = turned[:, i].reshape(2 * shell_size, ket_cols)
@@ -195,51 +201,36 @@
     )(nu, at, got)
 
 
-def transform_body(*refs, chunk, part, count, pieces):
+def transform_body(*refs, part, count, pieces):
     halves, panels = refs[:pieces], refs[pieces : pieces + count]
-    outs, held, sems = refs[pieces + count : -2], refs[-2], refs[-1]
-    depth, columns = panels[0].shape
-    rows = halves[0].shape[1]
-    copies = [
-        [
-            pltpu.make_async_copy(panel.at[:, pl.ds(start, chunk)], held.at[block, :, pl.ds(start, chunk)], sems.at[step, block])
-            for block, panel in enumerate(panels)
-        ]
-        for step, start in enumerate(range(0, columns, chunk))
-    ]
-    for row in copies:
-        for copy in row:
-            copy.start()
+    outs, gathered = refs[pieces + count : -1], refs[-1]
+    unused_dim, rows, lanes = halves[0].shape
+    columns = panels[0].shape[1]
+    for piece, half_ref in enumerate(halves):
+        for block in range(count):
+            gathered[piece * rows : (piece + 1) * rows, block * lanes : (block + 1) * lanes] = half_ref[block]
     for start in range(0, columns, part):
-        total = None
-        for block in range(count):
-            if start % chunk == 0:
-                copies[start // chunk][block].wait()
-            half = jnp.concatenate([half_ref[block] for half_ref in halves], axis=0)[:, :depth]
-            term = jnp.dot(half, held[block, :, start : start + part], preferred_element_type=jnp.float32)
-            total = term if total is None else total + term
+        panel = jnp.concatenate([panel_ref[:, start : start + part] for panel_ref in panels], axis=0)
+        total = jnp.dot(gathered[...], panel, preferred_element_type=jnp.float32)
         for piece, out_ref in enumerate(outs):
             out_ref[:, start : start + part] = total[piece * rows : (piece + 1) * rows].astype(out_ref.dtype)
 
 
-def transform(halves, panels, dtypes, chunk, part):
+def transform(halves, panels, dtypes, part):
     blocks, rows, lanes = halves[0].shape
     depth, columns = panels[0].shape
     pieces = len(halves)
 
     def body(*refs):
-        transform_body(*refs, chunk=chunk, part=part, count=blocks, pieces=pieces)
+        transform_body(*refs, part=part, count=blocks, pieces=pieces)
 
     return pl.pallas_call(
         body,
         out_shape=[jax.ShapeDtypeStruct((rows, columns), dtype) for dtype in dtypes],
-        in_specs=[pl.BlockSpec(memory_space=pltpu.VMEM)] * pieces + [pl.BlockSpec(memory_space=pl.ANY)] * blocks,
+        in_specs=[pl.BlockSpec(memory_space=pltpu.VMEM)] * (pieces + blocks),
         out_specs=[pl.BlockSpec(memory_space=pltpu.VMEM)] * pieces,
-        scratch_shapes=[
-            pltpu.VMEM((blocks, depth, columns), jnp.bfloat16),
-            pltpu.SemaphoreType.DMA((columns // chunk, blocks)),
-        ],
-        compiler_params=pltpu.CompilerParams(vmem_limit_bytes=60 * 1024 * 1024),
+        scratch_shapes=[pltpu.VMEM((pieces * rows, blocks * lanes), jnp.bfloat16)],
+        compiler_params=pltpu.CompilerParams(vmem_limit_bytes=24 * 1024 * 1024),
         cost_estimate=pl.CostEstimate(
             flops=2 * pieces * rows * blocks * depth * columns, bytes_accessed=8 * 10**6, transcendentals=0
         ),
@@ -257,10 +248,11 @@
     ket_owned = ket_cols // device_count
     swap = [(0, 1), (1, 0)]
 
+    filled = jnp.pad(vir_coef, ((0, 2 * shell_size - depth), (0, 0)))
     diagonal = [(i, 3 - i) for i in range(4)]
-    by_near = lax.ppermute(vir_coef, NEAR, swap)
-    by_row = lax.ppermute(vir_coef, ROW, swap)
-    by_col = lax.ppermute(vir_coef, COL, swap)
+    by_near = lax.ppermute(filled, NEAR, swap)
+    by_row = lax.ppermute(filled, ROW, swap)
+    by_col = lax.ppermute(filled, COL, swap)
 
     flags = live_flags.reshape(device_count, slot_count)
     rank = jnp.cumsum(flags, axis=1) - 1
@@ -278,13 +270,13 @@
     own, to_core, to_far, to_both = sum_shells(shell_list(nu).reshape(-1), at, got, shell_size, shell_count, depth)
     own, near_row = lax.optimization_barrier((own, near_row))
     all_three = lax.ppermute(near_row, COL, swap)
-    panels = [vir_coef, by_col, by_row, row_col, by_near, near_col, near_row, all_three]
+    panels = [filled, by_col, by_row, row_col, by_near, near_col, near_row, all_three]
     from_far = lax.ppermute(to_far, FAR, swap)
     from_both = lax.ppermute(to_both, (FAR, CORE), diagonal)
     from_core = lax.ppermute(to_core, CORE, swap)
     wide, narrow = jnp.float32, jnp.bfloat16
     own_part, own_peer, far_part, far_peer = transform(
-        [own, from_core, from_far, from_both], panels, [wide, narrow, wide, narrow], 1024, 512
+        [own, from_core, from_far, from_both], panels, [wide, narrow, wide, narrow], 512
     )
     far_peer = lax.ppermute(far_peer, CORE, swap)
     far_part = (far_part + far_peer.astype(jnp.float32)).astype(jnp.bfloat16)

time: 105 us -> 96.8 us (0.922)
  Pallas kernels: 23.3 us -> 18.2 us
  starting transfers between devices: 20 us -> 17.2 us
  other arithmetic: 4.05 us -> 1.78 us
  waiting for transfers between devices: 54.5 us -> 56.4 us
    ppermute x1, waiting for transfers between devices: 7.01 us -> 0.01 us  [on_device(): from_far = lax.ppermute(to_far, FAR, swap)]
    ppermute x1, waiting for transfers between devices: 1.19 us -> 7.71 us  [on_device(): near_col = lax.ppermute(by_col, NEAR, swap)]
    pallas_call x1, Pallas kernels: 7.86 us -> 3.63 us  [transform(): pl.pallas_call(body, out_shape=[jax.ShapeDtypeStruct((rows, columns), dty...]
    ppermute x3, waiting for transfers between devices: 3.82 us -> 6.45 us  [the longest x1 5.65 us: on_device(): by_near = lax.ppermute(filled, NEAR, swap)]
    ppermute x1, waiting for transfers between devices: 2.03 us -> 4.41 us  [on_device(): from_both = lax.ppermute(to_both, (FAR, CORE), diagonal)]
    ppermute x1, starting transfers between devices: 1.83 us -> 0.01 us  [on_device(): near_col = lax.ppermute(by_col, NEAR, swap)]
    ppermute x1, starting transfers between devices: 0.02 us -> 1.71 us  [on_device(): row_col = lax.ppermute(by_row, COL, swap)]
    ppermute x1, starting transfers between devices: 2.01 us -> 0.36 us  [on_device(): from_both = lax.ppermute(to_both, (FAR, CORE), diagonal)]
  transfers between devices with their start and end apart: 14 -> 14, of which waited for: 11 -> 9; matrix products, arithmetic and copies ran while one was open for 2% -> 2% of each run, Pallas kernels for 15% -> 15%
where the time goes in v4:
time: 96.8 us; the launch traced here: 96.5 us
  waiting for transfers between devices  56.4 us (58%)
  Pallas kernels  18.2 us (19%)
  starting transfers between devices  17.2 us (18%)
  local copies, waits for them, and re-layouts  2.73 us (3%)
  other arithmetic  1.78 us (2%)
    ppermute x1, waiting for transfers between devices, on_device(): taken = lax.ppermute(far_part, FAR, swap)  18.6 us
    all_to_all x1, waiting for transfers between devices, on_device(): got = lax.all_to_all(quarter, AXES, split_axis=0, concat_axis=0, tiled=True)  14.4 us
    pallas_call x1, Pallas kernels, first_quarter(): pl.pallas_call(body, out_shape=jax.ShapeDtypeStruct(shape, jnp.bfloat16),...  9.2 us
    ppermute x1, waiting for transfers between devices, on_device(): near_col = lax.ppermute(by_col, NEAR, swap)  7.71 us
    ppermute x1, waiting for transfers between devices, on_device(): by_near = lax.ppermute(filled, NEAR, swap)  5.65 us
    ppermute x1, waiting for transfers between devices, on_device(): from_both = lax.ppermute(to_both, (FAR, CORE), diagonal)  4.41 us
    pallas_call x1, Pallas kernels, sum_shells(): pl.pallas_call(body, out_shape=[jax.ShapeDtypeStruct((sources // 4, rows,...  4.04 us
    pallas_call x1, Pallas kernels, transform(): pl.pallas_call(body, out_shape=[jax.ShapeDtypeStruct((rows, columns), dty...  3.63 us
  transfers between devices with their start and end apart: 14, of which 9 were waited for; matrix products, arithmetic and copies ran while one was open for 2% of the time, Pallas kernels for 15%

profile of v4, /device:TPU:0, one launch (start us, length us, event | category | flops | bytes accessed | tf_op | source)
XLA Modules:
  0.0 96.5 jit_solution(11434153099102917104)
XLA Ops:
  0.0 0.0 copy-start.1
  0.0 0.0 copy-start
  0.0 1.2 %pad.4.refs_4_ = bf16[128,3072]{1,0:T(8,128)(2,1)S(1)} pad(bf16[124,3072]{1,0:T(8,128)(2,1)} %param.7, bf16[]{:T(256)} %constant.41.clone.1), padding=0_4x0_0 | pad | bytes 1548290 | tf_op jit(solution)/shard_map/jit(_pad)/pad | solution.py:251
  1.2 3.0 %collective-permute-start.6 = (bf16[128,3072]{1,0:T(8,128)(2,1)S(1)}, bf16[128,3072]{1,0:T(8,128)(2,1)S(1)}, u32[]{:S(2)}, u32[]{:S(2)}) collective-permute-start(bf16[128,3072]{1,0:T(8,128)(2,1)S(1)} %pad.4.refs_4_), channel_id=1, source_target_pairs={{0,4},{4,0},{1,5},{5,1},{2,6},{6,2},{3,7},{7,3},{8,12},{12,8},{9,1... | collective-permute-start | bytes 2359304 | tf_op jit(solution)/shard_map/ppermute | solution.py:254
  4.3 1.5 %collective-permute-start.5 = (bf16[128,3072]{1,0:T(8,128)(2,1)S(1)}, bf16[128,3072]{1,0:T(8,128)(2,1)S(1)}, u32[]{:S(2)}, u32[]{:S(2)}) collective-permute-start(bf16[128,3072]{1,0:T(8,128)(2,1)S(1)} %pad.4.refs_4_), channel_id=1, source_target_pairs={{0,2},{2,0},{1,3},{3,1},{4,6},{6,4},{5,7},{7,5},{8,10},{10,8},{9,1... | collective-permute-start | bytes 2359304 | tf_op jit(solution)/shard_map/ppermute | solution.py:255
  5.8 1.6 %collective-permute-start = (bf16[128,3072]{1,0:T(8,128)(2,1)S(1)}, bf16[128,3072]{1,0:T(8,128)(2,1)}, u32[]{:S(2)}, u32[]{:S(2)}) collective-permute-start(bf16[128,3072]{1,0:T(8,128)(2,1)S(1)} %pad.4.refs_4_), channel_id=1, source_target_pairs={{0,8},{8,0},{1,9},{9,1},{2,10},{10,2},{3,11},{11,3},{4,12},{12,4},... | collective-permute-start | bytes 2359304 | tf_op jit(solution)/shard_map/ppermute | solution.py:253
  7.3 9.2 %first_quarter.1 = bf16[32,2,64,128]{3,2,1,0:T(8,128)(2,1)} custom-call(s32[1]{0:T(128)} %bitcast.5.refs_0_, s32[256]{0:T(256)} %refs_1_.1, s32[2,256]{1,0:T(2,128)} %refs_2_.1, bf16[32,3968]{1,0:T(8,128)(2,1)} %bitcast.8, bf16[8,64,64,64]{3,2,1,0:T(8,128)(2,1)} %refs_4_.1), custom_call_target="tpu_custom_call" | custom-call | flops 1000000000 | bytes 6000000 | tf_op jit(solution)/shard_map/first_quarter/pallas_call | solution.py:127
  16.5 3.0 %all-to-all-start = ((bf16[32,2,64,128]{3,2,1,0:T(8,128)(2,1)}), bf16[32,2,64,128]{3,2,1,0:T(8,128)(2,1)S(1)}, u32[]{:S(2)}, u32[]{:S(2)}) async-start(bf16[32,2,64,128]{3,2,1,0:T(8,128)(2,1)} %first_quarter.1), calls=%async_computation | async-start | bytes 2097152 | tf_op jit(solution)/shard_map/all_to_all | solution.py:264
  19.5 0.0 copy-done.1
  19.5 0.1 reduce_window_sum.13
  19.6 0.0 copy-done
  19.7 0.1 broadcast_in_dim.20
  19.7 0.1 copy.8
  19.8 0.1 copy.7
  19.9 0.2 reduce_window_sum.14
  20.0 0.1 copy.6
  20.2 0.1 copy.9
  20.3 0.1 copy.10
  20.4 0.6 broadcast_select_fusion.nu_ref
  21.0 0.8 collective-permute-done.6.refs_6_
  21.8 1.7 %collective-permute-start.7 = (bf16[128,3072]{1,0:T(8,128)(2,1)S(1)}, bf16[128,3072]{1,0:T(8,128)(2,1)}, u32[]{:S(2)}, u32[]{:S(2)}) collective-permute-start(bf16[128,3072]{1,0:T(8,128)(2,1)S(1)} %collective-permute-done.6.refs_6_), channel_id=1, source_target_pairs={{0,2},{2,0},{1,3},{3,1},{4,6},{6,4},{5,7},{7,5},{8,10},{10,8},{9,1... | collective-permute-start | bytes 2359304 | tf_op jit(solution)/shard_map/ppermute | solution.py:267
  23.5 5.7 %collective-permute-done.refs_8_ = bf16[128,3072]{1,0:T(8,128)(2,1)} collective-permute-done((bf16[128,3072]{1,0:T(8,128)(2,1)S(1)}, bf16[128,3072]{1,0:T(8,128)(2,1)}, u32[]{:S(2)}, u32[]{:S(2)}) %collective-permute-start) | collective-permute-done | bytes 786464 | tf_op jit(solution)/shard_map/ppermute | solution.py:253
  29.2 0.0 collective-permute-start.1
  29.2 1.3 %shell_list.1 = s32[32,4]{1,0:T(8,128)} custom-call(s32[32,4]{1,0:T(8,128)} %broadcast_select_fusion.nu_ref), custom_call_target="tpu_custom_call" | custom-call | flops 99999997952 | bytes 1000000 | tf_op jit(solution)/shard_map/shell_list/pallas_call | solution.py:57
  30.5 0.8 reshape.25.refs_0_
  31.3 0.1 stack.23.refs_1_
  31.4 0.0 collective-permute-done.5.refs_5_
  31.4 0.0 collective-permute-start.8
  31.4 14.4 %all-to-all-done.refs_2_ = bf16[32,2,64,128]{3,2,1,0:T(8,128)(2,1)S(1)} async-done(((bf16[32,2,64,128]{3,2,1,0:T(8,128)(2,1)}), bf16[32,2,64,128]{3,2,1,0:T(8,128)(2,1)S(1)}, u32[]{:S(2)}, u32[]{:S(2)}) %all-to-all-start) | async-done | bytes 1048608 | tf_op jit(solution)/shard_map/all_to_all | solution.py:264
  45.9 4.0 %sum_shells.1 = (bf16[8,64,128]{2,1,0:T(8,128)(2,1)S(1)}, bf16[8,64,128]{2,1,0:T(8,128)(2,1)S(1)}, bf16[8,64,128]{2,1,0:T(8,128)(2,1)S(1)}, bf16[8,64,128]{2,1,0:T(8,128)(2,1)S(1)}) custom-call(s32[128]{0:T(128)S(1)} %reshape.25.refs_0_, s32[5]{0:T(128)S(1)} %stack.23.refs_1_, bf16[32,2,64,128]{3,2,1,0:T(8,128)(2,1)S(1)} %all-to-all-done.refs_2_), custom_call_target="tpu_custom_call" | custom-call | flops 10000000 | bytes 4000000 | tf_op jit(solution)/shard_map/sum_shells/pallas_call | solution.py:188
  49.9 0.9 collective-permute-done.1.refs_10_
  50.8 1.3 %collective-permute-start.9 = (bf16[128,3072]{1,0:T(8,128)(2,1)}, bf16[128,3072]{1,0:T(8,128)(2,1)S(1)}, u32[]{:S(2)}, u32[]{:S(2)}) collective-permute-start(bf16[128,3072]{1,0:T(8,128)(2,1)} %collective-permute-done.1.refs_10_), channel_id=1, source_target_pairs={{0,2},{2,0},{1,3},{3,1},{4,6},{6,4},{5,7},{7,5},{8,10},{10,8},{9,1... | collective-permute-start | bytes 2359304 | tf_op jit(solution)/shard_map/ppermute | solution.py:272
  52.0 0.0 collective-permute-start.2
  52.0 2.4 %collective-permute-start.3 = (bf16[8,64,128]{2,1,0:T(8,128)(2,1)S(1)}, bf16[8,64,128]{2,1,0:T(8,128)(2,1)S(1)}, u32[]{:S(2)}, u32[]{:S(2)}) collective-permute-start(bf16[8,64,128]{2,1,0:T(8,128)(2,1)S(1)} %get-tuple-element.20), channel_id=1, source_target_pairs={{0,16},{16,0},{1,17},{17,1},{2,18},{18,2},{3,19},{19,3},{4,20},{20... | collective-permute-start | bytes 393224 | tf_op jit(solution)/shard_map/ppermute | solution.py:274
  54.4 0.0 collective-permute-done.7.refs_7_
  54.4 0.4 collective-permute-start.4
  54.8 7.7 %collective-permute-done.8.refs_9_ = bf16[128,3072]{1,0:T(8,128)(2,1)} collective-permute-done((bf16[128,3072]{1,0:T(8,128)(2,1)S(1)}, bf16[128,3072]{1,0:T(8,128)(2,1)}, u32[]{:S(2)}, u32[]{:S(2)}) %collective-permute-start.8) | collective-permute-done | bytes 786464 | tf_op jit(solution)/shard_map/ppermute | solution.py:266
  62.5 0.0 collective-permute-done.2.refs_1_
  62.5 0.0 collective-permute-done.3.refs_2_
  62.5 4.4 %collective-permute-done.4.refs_3_ = bf16[8,64,128]{2,1,0:T(8,128)(2,1)S(1)} collective-permute-done((bf16[8,64,128]{2,1,0:T(8,128)(2,1)S(1)}, bf16[8,64,128]{2,1,0:T(8,128)(2,1)S(1)}, u32[]{:S(2)}, u32[]{:S(2)}) %collective-permute-start.4) | collective-permute-done | bytes 131104 | tf_op jit(solution)/shard_map/ppermute | solution.py:275
  66.9 2.2 %collective-permute-done.9.refs_11_ = bf16[128,3072]{1,0:T(8,128)(2,1)S(1)} collective-permute-done((bf16[128,3072]{1,0:T(8,128)(2,1)}, bf16[128,3072]{1,0:T(8,128)(2,1)S(1)}, u32[]{:S(2)}, u32[]{:S(2)}) %collective-permute-start.9) | collective-permute-done | bytes 786464 | tf_op jit(solution)/shard_map/ppermute | solution.py:272
  69.2 3.6 %second_quarter.1 = (f32[64,3072]{1,0:T(8,128)S(1)}, bf16[64,3072]{1,0:T(8,128)(2,1)S(1)}, f32[64,3072]{1,0:T(8,128)S(1)}, bf16[64,3072]{1,0:T(8,128)(2,1)S(1)}) custom-call(bf16[8,64,128]{2,1,0:T(8,128)(2,1)S(1)} %get-tuple-element.18.refs_0_, bf16[8,64,128]{2,1,0:T(8,128)(2,1)S(1)} %collective-permute-done.2.refs_1_, ...), custom_call_target="tpu_custom_call" | custom-call | flops 1610612736 | bytes 8000000 | tf_op jit(solution)/shard_map/second_quarter/pallas_call | solution.py:227
  72.8 0.1 collective-permute-start.10
  72.9 1.7 %collective-permute-done.10 = bf16[64,3072]{1,0:T(8,128)(2,1)S(1)} collective-permute-done((bf16[64,3072]{1,0:T(8,128)(2,1)S(1)}, bf16[64,3072]{1,0:T(8,128)(2,1)S(1)}, u32[]{:S(2)}, u32[]{:S(2)}) %collective-permute-start.10) | collective-permute-done | bytes 393248 | tf_op jit(solution)/shard_map/ppermute | solution.py:281
  74.6 0.1 add_convert_fusion.1
  74.7 0.2 collective-permute-start.11
  74.9 2.1 %collective-permute-start.12 = (bf16[64,3072]{1,0:T(8,128)(2,1)S(1)}, bf16[64,3072]{1,0:T(8,128)(2,1)S(1)}, u32[]{:S(2)}, u32[]{:S(2)}) collective-permute-start(bf16[64,3072]{1,0:T(8,128)(2,1)S(1)} %add_convert_fusion.1), channel_id=1, source_target_pairs={{0,16},{16,0},{1,17},{17,1},{2,18},{18,2},{3,19},{19,3},{4,20},{20... | collective-permute-start | bytes 1179656 | tf_op jit(solution)/shard_map/ppermute | solution.py:284
  77.0 0.0 collective-permute-done.11
  77.0 18.6 %collective-permute-done.12 = bf16[64,3072]{1,0:T(8,128)(2,1)S(1)} collective-permute-done((bf16[64,3072]{1,0:T(8,128)(2,1)S(1)}, bf16[64,3072]{1,0:T(8,128)(2,1)S(1)}, u32[]{:S(2)}, u32[]{:S(2)}) %collective-permute-start.12) | collective-permute-done | bytes 393248 | tf_op jit(solution)/shard_map/ppermute | solution.py:284
  95.6 0.9 add_convert_fusion
  (5 shorter events, 0.1 us)
Async XLA Ops:
  0.0 19.5 %copy-start.1 = (s32[256]{0:T(256)S(1)}, s32[256]{0:T(256)}, u32[]{:S(2)}) copy-start(s32[256]{0:T(256)} %refs_1_.1) | copy-start | bytes 3076
  0.0 19.6 %copy-start = (s32[2,256]{1,0:T(2,128)S(1)}, s32[2,256]{1,0:T(2,128)}, u32[]{:S(2)}) copy-start(s32[2,256]{1,0:T(2,128)} %refs_2_.1) | copy-start | bytes 6148
  1.2 20.6 %collective-permute-start.6 = (bf16[128,3072]{1,0:T(8,128)(2,1)S(1)}, bf16[128,3072]{1,0:T(8,128)(2,1)S(1)}, u32[]{:S(2)}, u32[]{:S(2)}) collective-permute-start(bf16[128,3072]{1,0:T(8,128)(2,1)S(1)} %pad.4.refs_4_), channel_id=1, source_target_pairs={{0,4},{4,0},{1,5},{5,1},{2,6},{6,2},{3,7},{7,3},{8,12},{12,8},{9,1... | collective-permute-start | bytes 2359304 | tf_op jit(solution)/shard_map/ppermute | solution.py:254
  4.3 27.1 %collective-permute-start.5 = (bf16[128,3072]{1,0:T(8,128)(2,1)S(1)}, bf16[128,3072]{1,0:T(8,128)(2,1)S(1)}, u32[]{:S(2)}, u32[]{:S(2)}) collective-permute-start(bf16[128,3072]{1,0:T(8,128)(2,1)S(1)} %pad.4.refs_4_), channel_id=1, source_target_pairs={{0,2},{2,0},{1,3},{3,1},{4,6},{6,4},{5,7},{7,5},{8,10},{10,8},{9,1... | collective-permute-start | bytes 2359304 | tf_op jit(solution)/shard_map/ppermute | solution.py:255
  5.8 23.4 %collective-permute-start = (bf16[128,3072]{1,0:T(8,128)(2,1)S(1)}, bf16[128,3072]{1,0:T(8,128)(2,1)}, u32[]{:S(2)}, u32[]{:S(2)}) collective-permute-start(bf16[128,3072]{1,0:T(8,128)(2,1)S(1)} %pad.4.refs_4_), channel_id=1, source_target_pairs={{0,8},{8,0},{1,9},{9,1},{2,10},{10,2},{3,11},{11,3},{4,12},{12,4},... | collective-permute-start | bytes 2359304 | tf_op jit(solution)/shard_map/ppermute | solution.py:253
  16.5 29.3 %all-to-all-start = ((bf16[32,2,64,128]{3,2,1,0:T(8,128)(2,1)}), bf16[32,2,64,128]{3,2,1,0:T(8,128)(2,1)S(1)}, u32[]{:S(2)}, u32[]{:S(2)}) async-start(bf16[32,2,64,128]{3,2,1,0:T(8,128)(2,1)} %first_quarter.1), calls=%async_computation | async-start | bytes 2097152 | tf_op jit(solution)/shard_map/all_to_all | solution.py:264
  21.8 32.6 %collective-permute-start.7 = (bf16[128,3072]{1,0:T(8,128)(2,1)S(1)}, bf16[128,3072]{1,0:T(8,128)(2,1)}, u32[]{:S(2)}, u32[]{:S(2)}) collective-permute-start(bf16[128,3072]{1,0:T(8,128)(2,1)S(1)} %collective-permute-done.6.refs_6_), channel_id=1, source_target_pairs={{0,2},{2,0},{1,3},{3,1},{4,6},{6,4},{5,7},{7,5},{8,10},{10,8},{9,1... | collective-permute-start | bytes 2359304 | tf_op jit(solution)/shard_map/ppermute | solution.py:267
  29.2 21.6 %collective-permute-start.1 = (bf16[128,3072]{1,0:T(8,128)(2,1)}, bf16[128,3072]{1,0:T(8,128)(2,1)}, u32[]{:S(2)}, u32[]{:S(2)}) collective-permute-start(bf16[128,3072]{1,0:T(8,128)(2,1)} %collective-permute-done.refs_8_), channel_id=1, source_target_pairs={{0,4},{4,0},{1,5},{5,1},{2,6},{6,2},{3,7},{7,3},{8,12},{12,8},{9,1... | collective-permute-start | bytes 2359304 | tf_op jit(solution)/shard_map/ppermute | solution.py:265
  31.4 31.1 %collective-permute-start.8 = (bf16[128,3072]{1,0:T(8,128)(2,1)S(1)}, bf16[128,3072]{1,0:T(8,128)(2,1)}, u32[]{:S(2)}, u32[]{:S(2)}) collective-permute-start(bf16[128,3072]{1,0:T(8,128)(2,1)S(1)} %collective-permute-done.5.refs_5_), channel_id=1, source_target_pairs={{0,8},{8,0},{1,9},{9,1},{2,10},{10,2},{3,11},{11,3},{4,12},{12,4},... | collective-permute-start | bytes 2359304 | tf_op jit(solution)/shard_map/ppermute | solution.py:266
  50.8 18.4 %collective-permute-start.9 = (bf16[128,3072]{1,0:T(8,128)(2,1)}, bf16[128,3072]{1,0:T(8,128)(2,1)S(1)}, u32[]{:S(2)}, u32[]{:S(2)}) collective-permute-start(bf16[128,3072]{1,0:T(8,128)(2,1)} %collective-permute-done.1.refs_10_), channel_id=1, source_target_pairs={{0,2},{2,0},{1,3},{3,1},{4,6},{6,4},{5,7},{7,5},{8,10},{10,8},{9,1... | collective-permute-start | bytes 2359304 | tf_op jit(solution)/shard_map/ppermute | solution.py:272
  52.0 10.5 %collective-permute-start.2 = (bf16[8,64,128]{2,1,0:T(8,128)(2,1)S(1)}, bf16[8,64,128]{2,1,0:T(8,128)(2,1)S(1)}, u32[]{:S(2)}, u32[]{:S(2)}) collective-permute-start(bf16[8,64,128]{2,1,0:T(8,128)(2,1)S(1)} %get-tuple-element.19), channel_id=1, source_target_pairs={{0,1},{1,0},{2,3},{3,2},{4,5},{5,4},{6,7},{7,6},{8,9},{9,8},{10,11... | collective-permute-start | bytes 393224 | tf_op jit(solution)/shard_map/ppermute | solution.py:276
  52.0 10.5 %collective-permute-start.3 = (bf16[8,64,128]{2,1,0:T(8,128)(2,1)S(1)}, bf16[8,64,128]{2,1,0:T(8,128)(2,1)S(1)}, u32[]{:S(2)}, u32[]{:S(2)}) collective-permute-start(bf16[8,64,128]{2,1,0:T(8,128)(2,1)S(1)} %get-tuple-element.20), channel_id=1, source_target_pairs={{0,16},{16,0},{1,17},{17,1},{2,18},{18,2},{3,19},{19,3},{4,20},{20... | collective-permute-start | bytes 393224 | tf_op jit(solution)/shard_map/ppermute | solution.py:274
  54.4 12.5 %collective-permute-start.4 = (bf16[8,64,128]{2,1,0:T(8,128)(2,1)S(1)}, bf16[8,64,128]{2,1,0:T(8,128)(2,1)S(1)}, u32[]{:S(2)}, u32[]{:S(2)}) collective-permute-start(bf16[8,64,128]{2,1,0:T(8,128)(2,1)S(1)} %get-tuple-element.21), channel_id=1, source_target_pairs={{0,17},{1,16},{16,1},{17,0},{2,19},{3,18},{18,3},{19,2},{4,21},{5,... | collective-permute-start | bytes 393224 | tf_op jit(solution)/shard_map/ppermute | solution.py:275
  72.8 1.8 %collective-permute-start.10 = (bf16[64,3072]{1,0:T(8,128)(2,1)S(1)}, bf16[64,3072]{1,0:T(8,128)(2,1)S(1)}, u32[]{:S(2)}, u32[]{:S(2)}) collective-permute-start(bf16[64,3072]{1,0:T(8,128)(2,1)S(1)} %get-tuple-element.26), channel_id=1, source_target_pairs={{0,1},{1,0},{2,3},{3,2},{4,5},{5,4},{6,7},{7,6},{8,9},{9,8},{10,11... | collective-permute-start | bytes 1179656 | tf_op jit(solution)/shard_map/ppermute | solution.py:281
  74.7 2.4 %collective-permute-start.11 = (bf16[64,3072]{1,0:T(8,128)(2,1)S(1)}, bf16[64,3072]{1,0:T(8,128)(2,1)S(1)}, u32[]{:S(2)}, u32[]{:S(2)}) collective-permute-start(bf16[64,3072]{1,0:T(8,128)(2,1)S(1)} %get-tuple-element.27), channel_id=1, source_target_pairs={{0,1},{1,0},{2,3},{3,2},{4,5},{5,4},{6,7},{7,6},{8,9},{9,8},{10,11... | collective-permute-start | bytes 1179656 | tf_op jit(solution)/shard_map/ppermute | solution.py:285
  74.9 20.7 %collective-permute-start.12 = (bf16[64,3072]{1,0:T(8,128)(2,1)S(1)}, bf16[64,3072]{1,0:T(8,128)(2,1)S(1)}, u32[]{:S(2)}, u32[]{:S(2)}) collective-permute-start(bf16[64,3072]{1,0:T(8,128)(2,1)S(1)} %add_convert_fusion.1), channel_id=1, source_target_pairs={{0,16},{16,0},{1,17},{17,1},{2,18},{18,2},{3,19},{19,3},{4,20},{20... | collective-permute-start | bytes 1179656 | tf_op jit(solution)/shard_map/ppermute | solution.py:284

commit v5 on v4

--- a/solution.py
+++ b/solution.py
@@ -163,7 +163,7 @@
                 acc_ref[at] = acc_ref[at] + value
         return carry
 
-    lax.fori_loop(0, sources, add, 0)
+    lax.fori_loop(0, sources, add, 0, unroll=8)
     step = lanes - depth
     for piece, out_ref in enumerate(outs):
         for spot in range(out_ref.shape[0]):

time: 96.8 us -> 96 us (level)
  Pallas kernels: 18.2 us -> 16.2 us
    ppermute x1, waiting for transfers between devices: 0.87 us -> 2.84 us  [on_device(): near_row = lax.ppermute(by_near, ROW, swap)]
    pallas_call x1, Pallas kernels: 4.04 us -> 2.06 us  [sum_shells(): pl.pallas_call(body, out_shape=[jax.ShapeDtypeStruct((sources // 4, rows,...]
  transfers between devices with their start and end apart: 14 -> 14, of which waited for: 9 -> 9; matrix products, arithmetic and copies ran while one was open for 2% -> 2% of each run, Pallas kernels for 15% -> 13%
where the time goes in v5:
time: 96 us; the launch traced here: 95.7 us
  waiting for transfers between devices  57.3 us (60%)
  starting transfers between devices  17.5 us (18%)
  Pallas kernels  16.2 us (17%)
  local copies, waits for them, and re-layouts  2.73 us (3%)
  other arithmetic  1.78 us (2%)
    ppermute x1, waiting for transfers between devices, on_device(): taken = lax.ppermute(far_part, FAR, swap)  18.3 us
    all_to_all x1, waiting for transfers between devices, on_device(): got = lax.all_to_all(quarter, AXES, split_axis=0, concat_axis=0, tiled=True)  14.4 us
    pallas_call x1, Pallas kernels, first_quarter(): pl.pallas_call(body, out_shape=jax.ShapeDtypeStruct(shape, jnp.bfloat16),...  9.2 us
    ppermute x1, waiting for transfers between devices, on_device(): near_col = lax.ppermute(by_col, NEAR, swap)  7.71 us
    ppermute x1, waiting for transfers between devices, on_device(): by_near = lax.ppermute(filled, NEAR, swap)  5.65 us
    ppermute x1, waiting for transfers between devices, on_device(): from_both = lax.ppermute(to_both, (FAR, CORE), diagonal)  4.41 us
    pallas_call x1, Pallas kernels, transform(): pl.pallas_call(body, out_shape=[jax.ShapeDtypeStruct((rows, columns), dty...  3.63 us
    ppermute x1, starting transfers between devices, on_device(): by_row = lax.ppermute(filled, ROW, swap)  3.03 us
  transfers between devices with their start and end apart: 14, of which 9 were waited for; matrix products, arithmetic and copies ran while one was open for 2% of the time, Pallas kernels for 13%

profile of v5, /device:TPU:0, one launch (start us, length us, event | category | flops | bytes accessed | tf_op | source)
XLA Modules:
  0.0 95.7 jit_solution(722436155406729291)
XLA Ops:
  0.0 0.0 copy-start.1
  0.0 0.0 copy-start
  0.0 1.2 %pad.4.refs_4_ = bf16[128,3072]{1,0:T(8,128)(2,1)S(1)} pad(bf16[124,3072]{1,0:T(8,128)(2,1)} %param.7, bf16[]{:T(256)} %constant.41.clone.1), padding=0_4x0_0 | pad | bytes 1548290 | tf_op jit(solution)/shard_map/jit(_pad)/pad | solution.py:251
  1.2 3.0 %collective-permute-start.6 = (bf16[128,3072]{1,0:T(8,128)(2,1)S(1)}, bf16[128,3072]{1,0:T(8,128)(2,1)S(1)}, u32[]{:S(2)}, u32[]{:S(2)}) collective-permute-start(bf16[128,3072]{1,0:T(8,128)(2,1)S(1)} %pad.4.refs_4_), channel_id=1, source_target_pairs={{0,4},{4,0},{1,5},{5,1},{2,6},{6,2},{3,7},{7,3},{8,12},{12,8},{9,1... | collective-permute-start | bytes 2359304 | tf_op jit(solution)/shard_map/ppermute | solution.py:254
  4.3 1.5 %collective-permute-start.5 = (bf16[128,3072]{1,0:T(8,128)(2,1)S(1)}, bf16[128,3072]{1,0:T(8,128)(2,1)S(1)}, u32[]{:S(2)}, u32[]{:S(2)}) collective-permute-start(bf16[128,3072]{1,0:T(8,128)(2,1)S(1)} %pad.4.refs_4_), channel_id=1, source_target_pairs={{0,2},{2,0},{1,3},{3,1},{4,6},{6,4},{5,7},{7,5},{8,10},{10,8},{9,1... | collective-permute-start | bytes 2359304 | tf_op jit(solution)/shard_map/ppermute | solution.py:255
  5.8 1.6 %collective-permute-start = (bf16[128,3072]{1,0:T(8,128)(2,1)S(1)}, bf16[128,3072]{1,0:T(8,128)(2,1)}, u32[]{:S(2)}, u32[]{:S(2)}) collective-permute-start(bf16[128,3072]{1,0:T(8,128)(2,1)S(1)} %pad.4.refs_4_), channel_id=1, source_target_pairs={{0,8},{8,0},{1,9},{9,1},{2,10},{10,2},{3,11},{11,3},{4,12},{12,4},... | collective-permute-start | bytes 2359304 | tf_op jit(solution)/shard_map/ppermute | solution.py:253
  7.3 9.2 %first_quarter.1 = bf16[32,2,64,128]{3,2,1,0:T(8,128)(2,1)} custom-call(s32[1]{0:T(128)} %bitcast.5.refs_0_, s32[256]{0:T(256)} %refs_1_.1, s32[2,256]{1,0:T(2,128)} %refs_2_.1, bf16[32,3968]{1,0:T(8,128)(2,1)} %bitcast.8, bf16[8,64,64,64]{3,2,1,0:T(8,128)(2,1)} %refs_4_.1), custom_call_target="tpu_custom_call" | custom-call | flops 1000000000 | bytes 6000000 | tf_op jit(solution)/shard_map/first_quarter/pallas_call | solution.py:127
  16.5 3.0 %all-to-all-start = ((bf16[32,2,64,128]{3,2,1,0:T(8,128)(2,1)}), bf16[32,2,64,128]{3,2,1,0:T(8,128)(2,1)S(1)}, u32[]{:S(2)}, u32[]{:S(2)}) async-start(bf16[32,2,64,128]{3,2,1,0:T(8,128)(2,1)} %first_quarter.1), calls=%async_computation | async-start | bytes 2097152 | tf_op jit(solution)/shard_map/all_to_all | solution.py:264
  19.5 0.0 copy-done.1
  19.5 0.1 reduce_window_sum.13
  19.6 0.0 copy-done
  19.7 0.1 broadcast_in_dim.20
  19.7 0.1 copy.8
  19.8 0.1 copy.7
  19.9 0.2 reduce_window_sum.14
  20.0 0.1 copy.6
  20.2 0.1 copy.9
  20.3 0.1 copy.10
  20.4 0.6 broadcast_select_fusion.nu_ref
  21.0 0.8 collective-permute-done.6.refs_6_
  21.8 1.7 %collective-permute-start.7 = (bf16[128,3072]{1,0:T(8,128)(2,1)S(1)}, bf16[128,3072]{1,0:T(8,128)(2,1)}, u32[]{:S(2)}, u32[]{:S(2)}) collective-permute-start(bf16[128,3072]{1,0:T(8,128)(2,1)S(1)} %collective-permute-done.6.refs_6_), channel_id=1, source_target_pairs={{0,2},{2,0},{1,3},{3,1},{4,6},{6,4},{5,7},{7,5},{8,10},{10,8},{9,1... | collective-permute-start | bytes 2359304 | tf_op jit(solution)/shard_map/ppermute | solution.py:267
  23.5 5.7 %collective-permute-done.refs_8_ = bf16[128,3072]{1,0:T(8,128)(2,1)} collective-permute-done((bf16[128,3072]{1,0:T(8,128)(2,1)S(1)}, bf16[128,3072]{1,0:T(8,128)(2,1)}, u32[]{:S(2)}, u32[]{:S(2)}) %collective-permute-start) | collective-permute-done | bytes 786464 | tf_op jit(solution)/shard_map/ppermute | solution.py:253
  29.2 0.0 collective-permute-start.1
  29.2 1.3 %shell_list.1 = s32[32,4]{1,0:T(8,128)} custom-call(s32[32,4]{1,0:T(8,128)} %broadcast_select_fusion.nu_ref), custom_call_target="tpu_custom_call" | custom-call | flops 99999997952 | bytes 1000000 | tf_op jit(solution)/shard_map/shell_list/pallas_call | solution.py:57
  30.5 0.8 reshape.25.refs_0_
  31.3 0.1 stack.23.refs_1_
  31.4 0.0 collective-permute-done.5.refs_5_
  31.4 0.0 collective-permute-start.8
  31.4 14.4 %all-to-all-done.refs_2_ = bf16[32,2,64,128]{3,2,1,0:T(8,128)(2,1)S(1)} async-done(((bf16[32,2,64,128]{3,2,1,0:T(8,128)(2,1)}), bf16[32,2,64,128]{3,2,1,0:T(8,128)(2,1)S(1)}, u32[]{:S(2)}, u32[]{:S(2)}) %all-to-all-start) | async-done | bytes 1048608 | tf_op jit(solution)/shard_map/all_to_all | solution.py:264
  45.9 2.1 %sum_shells.1 = (bf16[8,64,128]{2,1,0:T(8,128)(2,1)S(1)}, bf16[8,64,128]{2,1,0:T(8,128)(2,1)S(1)}, bf16[8,64,128]{2,1,0:T(8,128)(2,1)S(1)}, bf16[8,64,128]{2,1,0:T(8,128)(2,1)S(1)}) custom-call(s32[128]{0:T(128)S(1)} %reshape.25.refs_0_, s32[5]{0:T(128)S(1)} %stack.23.refs_1_, bf16[32,2,64,128]{3,2,1,0:T(8,128)(2,1)S(1)} %all-to-all-done.refs_2_), custom_call_target="tpu_custom_call" | custom-call | flops 10000000 | bytes 4000000 | tf_op jit(solution)/shard_map/sum_shells/pallas_call | solution.py:188
  47.9 2.8 %collective-permute-done.1.refs_10_ = bf16[128,3072]{1,0:T(8,128)(2,1)} collective-permute-done((bf16[128,3072]{1,0:T(8,128)(2,1)}, bf16[128,3072]{1,0:T(8,128)(2,1)}, u32[]{:S(2)}, u32[]{:S(2)}) %collective-permute-start.1) | collective-permute-done | bytes 786464 | tf_op jit(solution)/shard_map/ppermute | solution.py:265
  50.8 1.3 %collective-permute-start.9 = (bf16[128,3072]{1,0:T(8,128)(2,1)}, bf16[128,3072]{1,0:T(8,128)(2,1)S(1)}, u32[]{:S(2)}, u32[]{:S(2)}) collective-permute-start(bf16[128,3072]{1,0:T(8,128)(2,1)} %collective-permute-done.1.refs_10_), channel_id=1, source_target_pairs={{0,2},{2,0},{1,3},{3,1},{4,6},{6,4},{5,7},{7,5},{8,10},{10,8},{9,1... | collective-permute-start | bytes 2359304 | tf_op jit(solution)/shard_map/ppermute | solution.py:272
  52.0 0.0 collective-permute-start.2
  52.0 2.4 %collective-permute-start.3 = (bf16[8,64,128]{2,1,0:T(8,128)(2,1)S(1)}, bf16[8,64,128]{2,1,0:T(8,128)(2,1)S(1)}, u32[]{:S(2)}, u32[]{:S(2)}) collective-permute-start(bf16[8,64,128]{2,1,0:T(8,128)(2,1)S(1)} %get-tuple-element.20), channel_id=1, source_target_pairs={{0,16},{16,0},{1,17},{17,1},{2,18},{18,2},{3,19},{19,3},{4,20},{20... | collective-permute-start | bytes 393224 | tf_op jit(solution)/shard_map/ppermute | solution.py:274
  54.4 0.0 collective-permute-done.7.refs_7_
  54.4 0.4 collective-permute-start.4
  54.8 7.7 %collective-permute-done.8.refs_9_ = bf16[128,3072]{1,0:T(8,128)(2,1)} collective-permute-done((bf16[128,3072]{1,0:T(8,128)(2,1)S(1)}, bf16[128,3072]{1,0:T(8,128)(2,1)}, u32[]{:S(2)}, u32[]{:S(2)}) %collective-permute-start.8) | collective-permute-done | bytes 786464 | tf_op jit(solution)/shard_map/ppermute | solution.py:266
  62.5 0.0 collective-permute-done.2.refs_1_
  62.5 0.0 collective-permute-done.3.refs_2_
  62.5 4.4 %collective-permute-done.4.refs_3_ = bf16[8,64,128]{2,1,0:T(8,128)(2,1)S(1)} collective-permute-done((bf16[8,64,128]{2,1,0:T(8,128)(2,1)S(1)}, bf16[8,64,128]{2,1,0:T(8,128)(2,1)S(1)}, u32[]{:S(2)}, u32[]{:S(2)}) %collective-permute-start.4) | collective-permute-done | bytes 131104 | tf_op jit(solution)/shard_map/ppermute | solution.py:275
  66.9 1.5 %collective-permute-done.9.refs_11_ = bf16[128,3072]{1,0:T(8,128)(2,1)S(1)} collective-permute-done((bf16[128,3072]{1,0:T(8,128)(2,1)}, bf16[128,3072]{1,0:T(8,128)(2,1)S(1)}, u32[]{:S(2)}, u32[]{:S(2)}) %collective-permute-start.9) | collective-permute-done | bytes 786464 | tf_op jit(solution)/shard_map/ppermute | solution.py:272
  68.4 3.6 %second_quarter.1 = (f32[64,3072]{1,0:T(8,128)S(1)}, bf16[64,3072]{1,0:T(8,128)(2,1)S(1)}, f32[64,3072]{1,0:T(8,128)S(1)}, bf16[64,3072]{1,0:T(8,128)(2,1)S(1)}) custom-call(bf16[8,64,128]{2,1,0:T(8,128)(2,1)S(1)} %get-tuple-element.18.refs_0_, bf16[8,64,128]{2,1,0:T(8,128)(2,1)S(1)} %collective-permute-done.2.refs_1_, ...), custom_call_target="tpu_custom_call" | custom-call | flops 1610612736 | bytes 8000000 | tf_op jit(solution)/shard_map/second_quarter/pallas_call | solution.py:227
  72.0 0.1 collective-permute-start.10
  72.1 1.7 %collective-permute-done.10 = bf16[64,3072]{1,0:T(8,128)(2,1)S(1)} collective-permute-done((bf16[64,3072]{1,0:T(8,128)(2,1)S(1)}, bf16[64,3072]{1,0:T(8,128)(2,1)S(1)}, u32[]{:S(2)}, u32[]{:S(2)}) %collective-permute-start.10) | collective-permute-done | bytes 393248 | tf_op jit(solution)/shard_map/ppermute | solution.py:281
  73.8 0.1 add_convert_fusion.1
  73.9 0.2 collective-permute-start.11
  74.1 2.4 %collective-permute-start.12 = (bf16[64,3072]{1,0:T(8,128)(2,1)S(1)}, bf16[64,3072]{1,0:T(8,128)(2,1)S(1)}, u32[]{:S(2)}, u32[]{:S(2)}) collective-permute-start(bf16[64,3072]{1,0:T(8,128)(2,1)S(1)} %add_convert_fusion.1), channel_id=1, source_target_pairs={{0,16},{16,0},{1,17},{17,1},{2,18},{18,2},{3,19},{19,3},{4,20},{20... | collective-permute-start | bytes 1179656 | tf_op jit(solution)/shard_map/ppermute | solution.py:284
  76.5 0.0 collective-permute-done.11
  76.5 18.3 %collective-permute-done.12 = bf16[64,3072]{1,0:T(8,128)(2,1)S(1)} collective-permute-done((bf16[64,3072]{1,0:T(8,128)(2,1)S(1)}, bf16[64,3072]{1,0:T(8,128)(2,1)S(1)}, u32[]{:S(2)}, u32[]{:S(2)}) %collective-permute-start.12) | collective-permute-done | bytes 393248 | tf_op jit(solution)/shard_map/ppermute | solution.py:284
  94.8 0.9 add_convert_fusion
  (5 shorter events, 0.1 us)
Async XLA Ops:
  0.0 19.5 %copy-start.1 = (s32[256]{0:T(256)S(1)}, s32[256]{0:T(256)}, u32[]{:S(2)}) copy-start(s32[256]{0:T(256)} %refs_1_.1) | copy-start | bytes 3076
  0.0 19.6 %copy-start = (s32[2,256]{1,0:T(2,128)S(1)}, s32[2,256]{1,0:T(2,128)}, u32[]{:S(2)}) copy-start(s32[2,256]{1,0:T(2,128)} %refs_2_.1) | copy-start | bytes 6148
  1.2 20.6 %collective-permute-start.6 = (bf16[128,3072]{1,0:T(8,128)(2,1)S(1)}, bf16[128,3072]{1,0:T(8,128)(2,1)S(1)}, u32[]{:S(2)}, u32[]{:S(2)}) collective-permute-start(bf16[128,3072]{1,0:T(8,128)(2,1)S(1)} %pad.4.refs_4_), channel_id=1, source_target_pairs={{0,4},{4,0},{1,5},{5,1},{2,6},{6,2},{3,7},{7,3},{8,12},{12,8},{9,1... | collective-permute-start | bytes 2359304 | tf_op jit(solution)/shard_map/ppermute | solution.py:254
  4.3 27.1 %collective-permute-start.5 = (bf16[128,3072]{1,0:T(8,128)(2,1)S(1)}, bf16[128,3072]{1,0:T(8,128)(2,1)S(1)}, u32[]{:S(2)}, u32[]{:S(2)}) collective-permute-start(bf16[128,3072]{1,0:T(8,128)(2,1)S(1)} %pad.4.refs_4_), channel_id=1, source_target_pairs={{0,2},{2,0},{1,3},{3,1},{4,6},{6,4},{5,7},{7,5},{8,10},{10,8},{9,1... | collective-permute-start | bytes 2359304 | tf_op jit(solution)/shard_map/ppermute | solution.py:255
  5.8 23.4 %collective-permute-start = (bf16[128,3072]{1,0:T(8,128)(2,1)S(1)}, bf16[128,3072]{1,0:T(8,128)(2,1)}, u32[]{:S(2)}, u32[]{:S(2)}) collective-permute-start(bf16[128,3072]{1,0:T(8,128)(2,1)S(1)} %pad.4.refs_4_), channel_id=1, source_target_pairs={{0,8},{8,0},{1,9},{9,1},{2,10},{10,2},{3,11},{11,3},{4,12},{12,4},... | collective-permute-start | bytes 2359304 | tf_op jit(solution)/shard_map/ppermute | solution.py:253
  16.5 29.3 %all-to-all-start = ((bf16[32,2,64,128]{3,2,1,0:T(8,128)(2,1)}), bf16[32,2,64,128]{3,2,1,0:T(8,128)(2,1)S(1)}, u32[]{:S(2)}, u32[]{:S(2)}) async-start(bf16[32,2,64,128]{3,2,1,0:T(8,128)(2,1)} %first_quarter.1), calls=%async_computation | async-start | bytes 2097152 | tf_op jit(solution)/shard_map/all_to_all | solution.py:264
  21.8 32.6 %collective-permute-start.7 = (bf16[128,3072]{1,0:T(8,128)(2,1)S(1)}, bf16[128,3072]{1,0:T(8,128)(2,1)}, u32[]{:S(2)}, u32[]{:S(2)}) collective-permute-start(bf16[128,3072]{1,0:T(8,128)(2,1)S(1)} %collective-permute-done.6.refs_6_), channel_id=1, source_target_pairs={{0,2},{2,0},{1,3},{3,1},{4,6},{6,4},{5,7},{7,5},{8,10},{10,8},{9,1... | collective-permute-start | bytes 2359304 | tf_op jit(solution)/shard_map/ppermute | solution.py:267
  29.2 21.6 %collective-permute-start.1 = (bf16[128,3072]{1,0:T(8,128)(2,1)}, bf16[128,3072]{1,0:T(8,128)(2,1)}, u32[]{:S(2)}, u32[]{:S(2)}) collective-permute-start(bf16[128,3072]{1,0:T(8,128)(2,1)} %collective-permute-done.refs_8_), channel_id=1, source_target_pairs={{0,4},{4,0},{1,5},{5,1},{2,6},{6,2},{3,7},{7,3},{8,12},{12,8},{9,1... | collective-permute-start | bytes 2359304 | tf_op jit(solution)/shard_map/ppermute | solution.py:265
  31.4 31.1 %collective-permute-start.8 = (bf16[128,3072]{1,0:T(8,128)(2,1)S(1)}, bf16[128,3072]{1,0:T(8,128)(2,1)}, u32[]{:S(2)}, u32[]{:S(2)}) collective-permute-start(bf16[128,3072]{1,0:T(8,128)(2,1)S(1)} %collective-permute-done.5.refs_5_), channel_id=1, source_target_pairs={{0,8},{8,0},{1,9},{9,1},{2,10},{10,2},{3,11},{11,3},{4,12},{12,4},... | collective-permute-start | bytes 2359304 | tf_op jit(solution)/shard_map/ppermute | solution.py:266
  50.8 17.6 %collective-permute-start.9 = (bf16[128,3072]{1,0:T(8,128)(2,1)}, bf16[128,3072]{1,0:T(8,128)(2,1)S(1)}, u32[]{:S(2)}, u32[]{:S(2)}) collective-permute-start(bf16[128,3072]{1,0:T(8,128)(2,1)} %collective-permute-done.1.refs_10_), channel_id=1, source_target_pairs={{0,2},{2,0},{1,3},{3,1},{4,6},{6,4},{5,7},{7,5},{8,10},{10,8},{9,1... | collective-permute-start | bytes 2359304 | tf_op jit(solution)/shard_map/ppermute | solution.py:272
  52.0 10.5 %collective-permute-start.2 = (bf16[8,64,128]{2,1,0:T(8,128)(2,1)S(1)}, bf16[8,64,128]{2,1,0:T(8,128)(2,1)S(1)}, u32[]{:S(2)}, u32[]{:S(2)}) collective-permute-start(bf16[8,64,128]{2,1,0:T(8,128)(2,1)S(1)} %get-tuple-element.19), channel_id=1, source_target_pairs={{0,1},{1,0},{2,3},{3,2},{4,5},{5,4},{6,7},{7,6},{8,9},{9,8},{10,11... | collective-permute-start | bytes 393224 | tf_op jit(solution)/shard_map/ppermute | solution.py:276
  52.0 10.5 %collective-permute-start.3 = (bf16[8,64,128]{2,1,0:T(8,128)(2,1)S(1)}, bf16[8,64,128]{2,1,0:T(8,128)(2,1)S(1)}, u32[]{:S(2)}, u32[]{:S(2)}) collective-permute-start(bf16[8,64,128]{2,1,0:T(8,128)(2,1)S(1)} %get-tuple-element.20), channel_id=1, source_target_pairs={{0,16},{16,0},{1,17},{17,1},{2,18},{18,2},{3,19},{19,3},{4,20},{20... | collective-permute-start | bytes 393224 | tf_op jit(solution)/shard_map/ppermute | solution.py:274
  54.4 12.5 %collective-permute-start.4 = (bf16[8,64,128]{2,1,0:T(8,128)(2,1)S(1)}, bf16[8,64,128]{2,1,0:T(8,128)(2,1)S(1)}, u32[]{:S(2)}, u32[]{:S(2)}) collective-permute-start(bf16[8,64,128]{2,1,0:T(8,128)(2,1)S(1)} %get-tuple-element.21), channel_id=1, source_target_pairs={{0,17},{1,16},{16,1},{17,0},{2,19},{3,18},{18,3},{19,2},{4,21},{5,... | collective-permute-start | bytes 393224 | tf_op jit(solution)/shard_map/ppermute | solution.py:275
  72.0 1.8 %collective-permute-start.10 = (bf16[64,3072]{1,0:T(8,128)(2,1)S(1)}, bf16[64,3072]{1,0:T(8,128)(2,1)S(1)}, u32[]{:S(2)}, u32[]{:S(2)}) collective-permute-start(bf16[64,3072]{1,0:T(8,128)(2,1)S(1)} %get-tuple-element.26), channel_id=1, source_target_pairs={{0,1},{1,0},{2,3},{3,2},{4,5},{5,4},{6,7},{7,6},{8,9},{9,8},{10,11... | collective-permute-start | bytes 1179656 | tf_op jit(solution)/shard_map/ppermute | solution.py:281
  73.9 2.6 %collective-permute-start.11 = (bf16[64,3072]{1,0:T(8,128)(2,1)S(1)}, bf16[64,3072]{1,0:T(8,128)(2,1)S(1)}, u32[]{:S(2)}, u32[]{:S(2)}) collective-permute-start(bf16[64,3072]{1,0:T(8,128)(2,1)S(1)} %get-tuple-element.27), channel_id=1, source_target_pairs={{0,1},{1,0},{2,3},{3,2},{4,5},{5,4},{6,7},{7,6},{8,9},{9,8},{10,11... | collective-permute-start | bytes 1179656 | tf_op jit(solution)/shard_map/ppermute | solution.py:285
  74.1 20.7 %collective-permute-start.12 = (bf16[64,3072]{1,0:T(8,128)(2,1)S(1)}, bf16[64,3072]{1,0:T(8,128)(2,1)S(1)}, u32[]{:S(2)}, u32[]{:S(2)}) collective-permute-start(bf16[64,3072]{1,0:T(8,128)(2,1)S(1)} %add_convert_fusion.1), channel_id=1, source_target_pairs={{0,16},{16,0},{1,17},{17,1},{2,18},{18,2},{3,19},{19,3},{4,20},{20... | collective-permute-start | bytes 1179656 | tf_op jit(solution)/shard_map/ppermute | solution.py:284
